TPU v7x, 32 devices: a whole 2x2x4 slice. The times are simulated.
32 devices in a mesh: ctx: 16 (over z, y, x), pp: 2 (over core).
Axes of the slice: x: 2, y: 2, z: 4, core: 2. Of those that a mesh axis runs over, the one named last changes fastest.
Arguments:
- inputs: bfloat16 [2, 2, 1024, 2048], P('pp', None, 'ctx'), may hold values from -6 to 6
- saved_keys: bfloat16 [2, 2, 1024, 512], P('pp', None, 'ctx'), may hold values from -6 to 6
- saved_values: bfloat16 [2, 2, 1024, 512], P('pp', None, 'ctx'), may hold values from -5 to 5
- query_gain: float32 [2, 2048], P('pp'), may hold values from 0.25 to 1.75
- first_grads: bfloat16 [2, 1024, 2048], P('pp', 'ctx'), may hold values from -5 to 5
- head_grads: bfloat16 [1, 1024, 2048], P(None, 'ctx'), may hold values from -5 to 5
- window: int32 [2, 4], P('pp'), may hold values from 1 to 7, as said below
- stride: int32 [2, 4], P('pp'), may hold values from 16 to 32, as said below
Outputs:
- grads_out: bfloat16 [2, 2, 1024, 2048], P('pp', None, 'ctx')
- key_grads: bfloat16 [2, 2, 1024, 512], P('pp', None, 'ctx')
- value_grads: bfloat16 [2, 2, 1024, 512], P('pp', None, 'ctx')
Inputs may be any that keep to these rules, and one draw needn't show every extreme that they name: `window`: every entry is 1 to 7; some entry equals 7 and some equals 1. `stride`: every entry is 16 or 32; both occur.
All inputs are finite; a program needn't handle non-finite values.
Results may differ from a plain program's by a relative error of at most 0.014.
Values may be sent and summed in bfloat16 or wider, within the bound.
A program may use at most 64 MiB of HBM per device.

v0:
```python
import jax
import jax.numpy as jnp
from jax import lax
from jax.sharding import PartitionSpec as P

BLK = 64
WIN = 7
STRIDE = 16
HEAD_DIM = 128


def shifted(block, axis, distance):
    devices = range(lax.axis_size(axis))
    route = [(i - distance, i) for i in devices if i - distance in devices]
    return lax.ppermute(block, axis, route)


def broadcast(array, axis, root):
    mine = lax.axis_index(axis) == root
    return lax.psum(jnp.where(mine, array, jnp.zeros_like(array)), axis)


def block_allowed(block, window, stride, summary_count):
    row_ids = jnp.arange(BLK, dtype=jnp.int32)
    query_pos = block * BLK + row_ids
    col_ids = jnp.arange(WIN * BLK, dtype=jnp.int32)
    key_block = block - WIN + 1 + col_ids // BLK
    key_pos = (block - WIN + 1) * BLK + col_ids
    local_ok = (key_block[None, None, :] >= 0) & (
        key_pos[None, None, :] <= query_pos[None, :, None]
    )
    local_ok = local_ok & ((block - key_block)[None, None, :] < window[:, None, None])
    strided_block = STRIDE * (jnp.arange(summary_count * BLK, dtype=jnp.int32) // BLK)
    strided_ok = strided_block[None, None, :] % stride[:, None, None] == 0
    strided_ok = strided_ok & (strided_block[None, None, :] <= block - window[:, None, None])
    heads = window.shape[0]
    strided_ok = jnp.broadcast_to(strided_ok, (heads, BLK, summary_count * BLK))
    return jnp.concatenate([local_ok, strided_ok], axis=2)


def head_backward(operands):
    query_h, key_h, value_h, grad_h, allowed_h = operands
    scale = HEAD_DIM ** (-0.5)
    group_size = query_h.shape[0] // allowed_h.shape[0]
    allowed_rows = jnp.tile(allowed_h, (group_size, 1))
    contract = (((1,), (1,)), ((), ()))
    scores = lax.dot_general(query_h, key_h, contract, preferred_element_type=jnp.float32) * scale
    scores = jnp.where(allowed_rows, scores, jnp.float32(-1e30))
    row_peak = jnp.max(scores, axis=1, keepdims=True)
    weights = jnp.exp(scores - row_peak)
    probs = weights / jnp.sum(weights, axis=1, keepdims=True)
    grad_prob = lax.dot_general(grad_h, value_h, contract, preferred_element_type=jnp.float32)
    row_delta = jnp.sum(probs * grad_prob, axis=1, keepdims=True)
    dscore = (probs * (grad_prob - row_delta) * scale).astype(jnp.bfloat16)
    probs_round = probs.astype(jnp.bfloat16)
    across = (((0,), (0,)), ((), ()))
    dquery = jnp.dot(dscore, key_h, preferred_element_type=jnp.float32)
    key_grad = lax.dot_general(dscore, query_h, across, preferred_element_type=jnp.float32)
    value_grad = lax.dot_general(probs_round, grad_h, across, preferred_element_type=jnp.float32)
    return (dquery, key_grad, value_grad)


def local_backward(inputs, gain, kv_all, grad_out, allowed):
    kv_heads = allowed.shape[0]
    rows, feat = inputs.shape
    group_size = feat // (kv_heads * HEAD_DIM)
    kv_width = kv_heads * HEAD_DIM
    key_count = kv_all.shape[0]
    queries = (inputs.astype(jnp.float32) * gain).astype(jnp.bfloat16)

    def regroup(matrix):
        shaped = matrix.reshape(rows, kv_heads, group_size, HEAD_DIM).transpose(1, 2, 0, 3)
        return shaped.reshape(kv_heads, group_size * rows, HEAD_DIM)

    key_heads = kv_all[:, :kv_width].reshape(key_count, kv_heads, HEAD_DIM).transpose(1, 0, 2)
    value_heads = kv_all[:, kv_width:].reshape(key_count, kv_heads, HEAD_DIM).transpose(1, 0, 2)
    dquery, key_grad, value_grad = lax.map(
        head_backward, (regroup(queries), key_heads, value_heads, regroup(grad_out), allowed)
    )
    dquery = (
        dquery.reshape(kv_heads, group_size, rows, HEAD_DIM)
        .transpose(2, 0, 1, 3)
        .reshape(rows, feat)
    )
    result = (grad_out.astype(jnp.float32) + gain * dquery).astype(jnp.bfloat16)
    key_grad = key_grad.transpose(1, 0, 2).reshape(key_count, kv_width)
    value_grad = value_grad.transpose(1, 0, 2).reshape(key_count, kv_width)
    return (result, jnp.concatenate([key_grad, value_grad], axis=1))


def pick_owned(combined, block_index):
    slot = jnp.minimum(block_index // STRIDE, combined.shape[0] - 1)
    owned_row = lax.dynamic_index_in_dim(combined, slot, 0, keepdims=False)
    return jnp.where(block_index % STRIDE == 0, owned_row, jnp.float32(0.0))


def body(inputs, saved_keys, saved_values, query_gain, first_grads, head_grads, window, stride):
    block_index = lax.axis_index("ctx")
    section_index = lax.axis_index("pp")
    section_count = lax.axis_size("pp")
    summary_count = lax.axis_size("ctx") // STRIDE
    tick_count = inputs.shape[1]
    kv_width = saved_keys.shape[-1]
    paired = jnp.concatenate([saved_keys[0], saved_values[0]], axis=-1)
    behind = [paired]
    for offset in range(1, WIN):
        behind.append(shifted(paired, "ctx", offset))
    nearby = jnp.stack(behind[::-1], axis=1)
    nearby = nearby.reshape(tick_count, WIN * BLK, 2 * kv_width)
    owners = [
        broadcast(paired, "ctx", owner_index * STRIDE) for owner_index in range(summary_count)
    ]
    summary = jnp.stack(owners, axis=1).reshape(tick_count, summary_count * BLK, 2 * kv_width)
    allowed = block_allowed(block_index, window[0], stride[0], summary_count)
    results = []
    finished = []
    previous = first_grads[0]
    for step_index in range(tick_count):
        if step_index == 0:
            grad_out = first_grads[0]
        else:
            incoming = shifted(previous, "pp", -1)
            grad_out = jnp.where(
                section_index == section_count - 1, head_grads[step_index - 1], incoming
            )
        kv_all = jnp.concatenate([nearby[step_index], summary[step_index]], axis=0)
        result, local_part = local_backward(
            inputs[0, step_index], query_gain[0], kv_all, grad_out, allowed
        )
        own_total = local_part[(WIN - 1) * BLK : WIN * BLK]
        for offset in range(1, WIN):
            start = (WIN - 1 - offset) * BLK
            piece = local_part[start : start + BLK].astype(jnp.bfloat16)
            own_total = own_total + shifted(piece, "ctx", -offset).astype(jnp.float32)
        summary_part = local_part[WIN * BLK :].reshape(summary_count, BLK, 2 * kv_width)
        combined = lax.psum(summary_part, "ctx")
        finished.append(own_total + pick_owned(combined, block_index))
        results.append(result)
        previous = result
    totals = jnp.stack(finished, axis=0)
    grads_out = jnp.stack(results, axis=0)[None]
    key_grads = totals[:, :, :kv_width].astype(jnp.bfloat16)[None]
    value_grads = totals[:, :, kv_width:].astype(jnp.bfloat16)[None]
    return (grads_out, key_grads, value_grads)


def solution(mesh):
    in_specs = (
        P("pp", None, "ctx", None),
        P("pp", None, "ctx", None),
        P("pp", None, "ctx", None),
        P("pp", None),
        P("pp", "ctx", None),
        P(None, "ctx", None),
        P("pp", None),
        P("pp", None),
    )
    out_specs = (P("pp", None, "ctx", None), P("pp", None, "ctx", None), P("pp", None, "ctx", None))
    return jax.shard_map(body, mesh=mesh, in_specs=in_specs, out_specs=out_specs, check_vma=False)
```

profile of v0, /device:TPU:0, one launch (start us, length us, event | category | flops | bytes accessed | tf_op | source)
XLA Modules:
  0.0 352.2 jit_solution(13070312808090891962)
XLA Ops:
  7.2 1.8 broadcast_select_fusion
  9.0 6.6 %collective-permute-start = (bf16[2,64,1024]{2,1,0:T(8,128)(2,1)}, bf16[2,64,1024]{2,1,0:T(8,128)(2,1)}, u32[]{:S(2)}, u32[]{:S(2)}) collective-permute-start(bf16[2,64,1024]{2,1,0:T(8,128)(2,1)} %get-tuple-element.214), channel_id=1, source_target_pairs={{0,12},{2,14},{4,16},{6,18},{8,20},{10,22},{12,24},{14,26},{16,28}... | collective-permute-start | bytes 786440 | tf_op jit(solution)/shard_map/ppermute | solution.py:15
  15.6 5.1 %collective-permute-start.1 = (bf16[2,64,1024]{2,1,0:T(8,128)(2,1)}, bf16[2,64,1024]{2,1,0:T(8,128)(2,1)}, u32[]{:S(2)}, u32[]{:S(2)}) collective-permute-start(bf16[2,64,1024]{2,1,0:T(8,128)(2,1)} %get-tuple-element.214), channel_id=1, source_target_pairs={{0,10},{2,12},{4,14},{6,16},{8,18},{10,20},{12,22},{14,24},{16,26}... | collective-permute-start | bytes 786440 | tf_op jit(solution)/shard_map/ppermute | solution.py:15
  20.7 2.8 collective-permute-start.2
  23.5 2.2 collective-permute-start.3
  25.7 2.4 collective-permute-start.4
  33.5 105.3 %all-reduce.4.cloned.1.call-done = bf16[2,64,1024]{2,1,0:T(8,128)(2,1)} async-done(((bf16[2,64,1024]{2,1,0:T(8,128)(2,1)}), bf16[2,64,1024]{2,1,0:T(8,128)(2,1)}) %all-reduce.4.cloned.1.call-update) | async-done | bytes 262160 | tf_op jit(solution)/shard_map/psum | solution.py:20
  139.8 3.4 collective-permute-start.5
  145.2 2.1 collective-permute-done.5
  150.8 18.0 %while.28 = (s32[]{:T(128)}, f32[4,256,128]{2,1,0:T(8,128)}, f32[4,512,128]{2,1,0:T(8,128)S(1)}, f32[4,512,128]{2,1,0:T(8,128)S(1)}, pred[4,64,512]{2,1,0:T(8,12...) while((s32[]{:T(128)}, f32[4,256,128]{2,1,0:T(8,128)}, ...), condition=%wide.region_5.6_spmd, body=%wide.region_1.5_spmd.sunk | while | flops 170130688 | bytes 6144105 | solution.py:77
  168.8 1.7 copy.76
  176.3 1.3 collective-permute-start.11
  177.6 1.3 collective-permute-start.12
  178.9 1.3 collective-permute-start.7
  181.0 1.4 collective-permute-start.6
  184.4 2.1 copy.47
  187.2 1.3 collective-permute-start.8
  193.4 20.1 %while.29 = (s32[]{:T(128)}, f32[4,256,128]{2,1,0:T(8,128)}, f32[4,512,128]{2,1,0:T(8,128)}, f32[4,512,128]{2,1,0:T(8,128)}, pred[4,64,512]{2,1,0:T(8,128)(4,1)S...) while((s32[]{:T(128)}, f32[4,256,128]{2,1,0:T(8,128)}, ...), condition=%wide.region_10.11_spmd, body=%wide.region_6.10_spmd.sunk | while | flops 170130688 | bytes 6144105 | solution.py:77
  213.5 1.4 bitcast_dynamic-update-slice_fusion.1
  215.1 1.3 copy-done
  217.2 1.4 copy.75
  218.9 1.8 convert.24
  220.8 1.3 collective-permute-start.9
  222.1 1.3 collective-permute-start.13
  224.3 1.3 collective-permute-start.14
  225.6 1.3 collective-permute-start.15
  226.9 1.3 collective-permute-start.16
  228.2 4.7 %collective-permute-done.9 = bf16[64,1024]{1,0:T(8,128)(2,1)S(1)} collective-permute-done((bf16[64,1024]{1,0:T(8,128)(2,1)S(1)}, bf16[64,1024]{1,0:T(8,128)(2,1)S(1)}, u32[]{:S(2)}, u32[]{:S(2)}) %collective-permute-start.9) | collective-permute-done | bytes 131104 | tf_op jit(solution)/shard_map/ppermute | solution.py:15
  232.9 1.3 collective-permute-start.17
  234.2 1.3 collective-permute-start.18
  235.5 106.5 %all-reduce.6.cloned.1.call-done = (f32[1,64,1024]{2,1,0:T(8,128)}, f32[1,64,1024]{2,1,0:T(8,128)}) async-done(((f32[1,64,1024]{2,1,0:T(8,128)}, f32[1,64,1024]{2,1,0:T(8,128)}), (f32[1,64,1024]{2,1,0:T(8,128)}, f32[1,64,1024]{2,1,0:T(8,128)})) %all-reduce.6.cloned.1.call-update) | async-done | bytes 524304 | tf_op jit(solution)/shard_map/psum | solution.py:136
  342.0 1.3 fusion.77
  (184 shorter events, 67.7 us)
Async XLA Ops:
  7.2 131.6 %all-reduce.4.cloned.1.call-start = ((), (), s32[]{:S(2)}) async-start(), calls=%async_computation | async-start | bytes 524288 | tf_op jit(solution)/shard_map/psum | solution.py:20
  9.0 130.7 %collective-permute-start = (bf16[2,64,1024]{2,1,0:T(8,128)(2,1)}, bf16[2,64,1024]{2,1,0:T(8,128)(2,1)}, u32[]{:S(2)}, u32[]{:S(2)}) collective-permute-start(bf16[2,64,1024]{2,1,0:T(8,128)(2,1)} %get-tuple-element.214), channel_id=1, source_target_pairs={{0,12},{2,14},{4,16},{6,18},{8,20},{10,22},{12,24},{14,26},{16,28}... | collective-permute-start | bytes 786440 | tf_op jit(solution)/shard_map/ppermute | solution.py:15
  15.6 128.5 %collective-permute-start.1 = (bf16[2,64,1024]{2,1,0:T(8,128)(2,1)}, bf16[2,64,1024]{2,1,0:T(8,128)(2,1)}, u32[]{:S(2)}, u32[]{:S(2)}) collective-permute-start(bf16[2,64,1024]{2,1,0:T(8,128)(2,1)} %get-tuple-element.214), channel_id=1, source_target_pairs={{0,10},{2,12},{4,14},{6,16},{8,18},{10,20},{12,22},{14,24},{16,26}... | collective-permute-start | bytes 786440 | tf_op jit(solution)/shard_map/ppermute | solution.py:15
  20.7 124.4 %collective-permute-start.2 = (bf16[2,64,1024]{2,1,0:T(8,128)(2,1)}, bf16[2,64,1024]{2,1,0:T(8,128)(2,1)S(1)}, u32[]{:S(2)}, u32[]{:S(2)}) collective-permute-start(bf16[2,64,1024]{2,1,0:T(8,128)(2,1)} %get-tuple-element.214), channel_id=1, source_target_pairs={{0,8},{2,10},{4,12},{6,14},{8,16},{10,18},{12,20},{14,22},{16,24},... | collective-permute-start | bytes 786440 | tf_op jit(solution)/shard_map/ppermute | solution.py:15
  23.5 121.6 %collective-permute-start.3 = (bf16[2,64,1024]{2,1,0:T(8,128)(2,1)}, bf16[2,64,1024]{2,1,0:T(8,128)(2,1)S(1)}, u32[]{:S(2)}, u32[]{:S(2)}) collective-permute-start(bf16[2,64,1024]{2,1,0:T(8,128)(2,1)} %get-tuple-element.214), channel_id=1, source_target_pairs={{0,6},{2,8},{4,10},{6,12},{8,14},{10,16},{12,18},{14,20},{16,22},{... | collective-permute-start | bytes 786440 | tf_op jit(solution)/shard_map/ppermute | solution.py:15
  25.7 119.4 %collective-permute-start.4 = (bf16[2,64,1024]{2,1,0:T(8,128)(2,1)}, bf16[2,64,1024]{2,1,0:T(8,128)(2,1)S(1)}, u32[]{:S(2)}, u32[]{:S(2)}) collective-permute-start(bf16[2,64,1024]{2,1,0:T(8,128)(2,1)} %get-tuple-element.214), channel_id=1, source_target_pairs={{0,4},{2,6},{4,8},{6,10},{8,12},{10,14},{12,16},{14,18},{16,20},{1... | collective-permute-start | bytes 786440 | tf_op jit(solution)/shard_map/ppermute | solution.py:15
  28.2 313.8 %all-reduce.6.cloned.1.call-start = ((), (), s32[]{:S(2)}) async-start(), calls=%async_computation.1 | async-start | bytes 1048576 | tf_op jit(solution)/shard_map/psum | solution.py:136
  29.6 2.2 copy-start.13
  33.4 113.9 %copy-start.9 = (bf16[1,2,64,512]{3,2,1,0:T(8,128)(2,1)S(1)}, bf16[1,2,64,512]{3,2,1,0:T(8,128)(2,1)}, u32[]{:S(2)}) copy-start(bf16[1,2,64,512]{3,2,1,0:T(8,128)(2,1)} %param.14) | copy-start | bytes 393220
  33.5 113.9 %copy-start.10 = (bf16[1,2,64,512]{3,2,1,0:T(8,128)(2,1)S(1)}, bf16[1,2,64,512]{3,2,1,0:T(8,128)(2,1)}, u32[]{:S(2)}) copy-start(bf16[1,2,64,512]{3,2,1,0:T(8,128)(2,1)} %param.13) | copy-start | bytes 393220
  139.8 7.5 %collective-permute-start.5 = (bf16[2,64,1024]{2,1,0:T(8,128)(2,1)}, bf16[2,64,1024]{2,1,0:T(8,128)(2,1)S(1)}, u32[]{:S(2)}, u32[]{:S(2)}) collective-permute-start(bf16[2,64,1024]{2,1,0:T(8,128)(2,1)} %get-tuple-element.214), channel_id=1, source_target_pairs={{0,2},{2,4},{4,6},{6,8},{8,10},{10,12},{12,14},{14,16},{16,18},{18... | collective-permute-start | bytes 786440 | tf_op jit(solution)/shard_map/ppermute | solution.py:15
  168.8 3.8 %copy-start.2 = (f32[4,512,128]{2,1,0:T(8,128)}, f32[4,512,128]{2,1,0:T(8,128)S(1)}, u32[]{:S(2)}) copy-start(f32[4,512,128]{2,1,0:T(8,128)S(1)} %get-tuple-element.104) | copy-start | bytes 3145732
  173.9 6.3 %copy-start.5 = (bf16[1,64,2048]{2,1,0:T(8,128)(2,1)S(1)}, bf16[1,64,2048]{2,1,0:T(8,128)(2,1)}, u32[]{:S(2)}) copy-start(bf16[1,64,2048]{2,1,0:T(8,128)(2,1)} %param.16) | copy-start | bytes 786436
  173.9 6.3 %copy-start.7 = (f32[64,2048]{1,0:T(8,128)S(1)}, f32[64,2048]{1,0:T(8,128)}, u32[]{:S(2)}) copy-start(f32[64,2048]{1,0:T(8,128)} %reshape.404) | copy-start | bytes 1572868
  174.1 8.3 %copy-start.6 = (f32[1,64,2048]{2,1,0:T(8,128)S(1)}, f32[1,64,2048]{2,1,0:T(8,128)}, u32[]{:S(2)}) copy-start(f32[1,64,2048]{2,1,0:T(8,128)} %reshape.403) | copy-start | bytes 1572868
  175.0 45.8 %collective-permute-start.10 = (bf16[64,1024]{1,0:T(8,128)(2,1)}, bf16[64,1024]{1,0:T(8,128)(2,1)}, u32[]{:S(2)}, u32[]{:S(2)}) collective-permute-start(bf16[64,1024]{1,0:T(8,128)(2,1)} %get-tuple-element.194), channel_id=1, source_target_pairs={{8,0},{10,2},{12,4},{14,6},{16,8},{18,10},{20,12},{22,14},{24,16},... | collective-permute-start | bytes 393224 | tf_op jit(solution)/shard_map/ppermute | solution.py:15
  176.3 45.8 %collective-permute-start.11 = (bf16[64,1024]{1,0:T(8,128)(2,1)}, bf16[64,1024]{1,0:T(8,128)(2,1)}, u32[]{:S(2)}, u32[]{:S(2)}) collective-permute-start(bf16[64,1024]{1,0:T(8,128)(2,1)} %get-tuple-element.193), channel_id=1, source_target_pairs={{10,0},{12,2},{14,4},{16,6},{18,8},{20,10},{22,12},{24,14},{26,16}... | collective-permute-start | bytes 393224 | tf_op jit(solution)/shard_map/ppermute | solution.py:15
  177.6 46.7 %collective-permute-start.12 = (bf16[64,1024]{1,0:T(8,128)(2,1)}, bf16[64,1024]{1,0:T(8,128)(2,1)}, u32[]{:S(2)}, u32[]{:S(2)}) collective-permute-start(bf16[64,1024]{1,0:T(8,128)(2,1)} %get-tuple-element.192), channel_id=1, source_target_pairs={{12,0},{14,2},{16,4},{18,6},{20,8},{22,10},{24,12},{26,14},{28,16}... | collective-permute-start | bytes 393224 | tf_op jit(solution)/shard_map/ppermute | solution.py:15
  178.9 46.7 %collective-permute-start.7 = (bf16[64,1024]{1,0:T(8,128)(2,1)}, bf16[64,1024]{1,0:T(8,128)(2,1)}, u32[]{:S(2)}, u32[]{:S(2)}) collective-permute-start(bf16[64,1024]{1,0:T(8,128)(2,1)} %get-tuple-element.191), channel_id=1, source_target_pairs={{2,0},{4,2},{6,4},{8,6},{10,8},{12,10},{14,12},{16,14},{18,16},{20... | collective-permute-start | bytes 393224 | tf_op jit(solution)/shard_map/ppermute | solution.py:15
  181.0 7.5 %copy-start.12 = (bf16[1,64,2048]{2,1,0:T(8,128)(2,1)S(1)}, bf16[1,64,2048]{2,1,0:T(8,128)(2,1)}, u32[]{:S(2)}) copy-start(bf16[1,64,2048]{2,1,0:T(8,128)(2,1)} %param.17) | copy-start | bytes 786436
  181.0 6.2 %collective-permute-start.6 = (bf16[64,2048]{1,0:T(8,128)(2,1)}, bf16[64,2048]{1,0:T(8,128)(2,1)}, u32[]{:S(2)}, u32[]{:S(2)}) collective-permute-start(bf16[64,2048]{1,0:T(8,128)(2,1)} %fusion.58), channel_id=1, source_target_pairs={{1,0},{3,2},{5,4},{7,6},{9,8},{11,10},{13,12},{15,14},{17,16},{19,... | collective-permute-start | bytes 786440 | tf_op jit(solution)/shard_map/ppermute | solution.py:15
  187.2 39.7 %collective-permute-start.8 = (bf16[64,1024]{1,0:T(8,128)(2,1)}, bf16[64,1024]{1,0:T(8,128)(2,1)}, u32[]{:S(2)}, u32[]{:S(2)}) collective-permute-start(bf16[64,1024]{1,0:T(8,128)(2,1)} %get-tuple-element.196), channel_id=1, source_target_pairs={{4,0},{6,2},{8,4},{10,6},{12,8},{14,10},{16,12},{18,14},{20,16},{2... | collective-permute-start | bytes 393224 | tf_op jit(solution)/shard_map/ppermute | solution.py:15
  190.5 2.9 copy-start.11
  218.9 1.9 copy-start.14
  218.9 4.5 %copy-start.8 = (bf16[1,64,2048]{2,1,0:T(8,128)(2,1)S(1)}, bf16[1,64,2048]{2,1,0:T(8,128)(2,1)}, u32[]{:S(2)}) copy-start(bf16[1,64,2048]{2,1,0:T(8,128)(2,1)} %fusion.56) | copy-start | bytes 786436
  220.8 12.1 %collective-permute-start.9 = (bf16[64,1024]{1,0:T(8,128)(2,1)S(1)}, bf16[64,1024]{1,0:T(8,128)(2,1)S(1)}, u32[]{:S(2)}, u32[]{:S(2)}) collective-permute-start(bf16[64,1024]{1,0:T(8,128)(2,1)S(1)} %copy-done.14), channel_id=1, source_target_pairs={{6,0},{8,2},{10,4},{12,6},{14,8},{16,10},{18,12},{20,14},{22,16},{... | collective-permute-start | bytes 393224 | tf_op jit(solution)/shard_map/ppermute | solution.py:15
  222.1 12.0 %collective-permute-start.13 = (bf16[64,1024]{1,0:T(8,128)(2,1)S(1)}, bf16[64,1024]{1,0:T(8,128)(2,1)S(1)}, u32[]{:S(2)}, u32[]{:S(2)}) collective-permute-start(bf16[64,1024]{1,0:T(8,128)(2,1)S(1)} %get-tuple-element.197), channel_id=1, source_target_pairs={{2,0},{4,2},{6,4},{8,6},{10,8},{12,10},{14,12},{16,14},{18,16},{20... | collective-permute-start | bytes 393224 | tf_op jit(solution)/shard_map/ppermute | solution.py:15
  224.3 119.1 %collective-permute-start.14 = (bf16[64,1024]{1,0:T(8,128)(2,1)S(1)}, bf16[64,1024]{1,0:T(8,128)(2,1)S(1)}, u32[]{:S(2)}, u32[]{:S(2)}) collective-permute-start(bf16[64,1024]{1,0:T(8,128)(2,1)S(1)} %get-tuple-element.202), channel_id=1, source_target_pairs={{4,0},{6,2},{8,4},{10,6},{12,8},{14,10},{16,12},{18,14},{20,16},{2... | collective-permute-start | bytes 393224 | tf_op jit(solution)/shard_map/ppermute | solution.py:15
  225.6 117.8 %collective-permute-start.15 = (bf16[64,1024]{1,0:T(8,128)(2,1)S(1)}, bf16[64,1024]{1,0:T(8,128)(2,1)S(1)}, u32[]{:S(2)}, u32[]{:S(2)}) collective-permute-start(bf16[64,1024]{1,0:T(8,128)(2,1)S(1)} %get-tuple-element.201), channel_id=1, source_target_pairs={{6,0},{8,2},{10,4},{12,6},{14,8},{16,10},{18,12},{20,14},{22,16},{... | collective-permute-start | bytes 393224 | tf_op jit(solution)/shard_map/ppermute | solution.py:15
  226.9 116.5 %collective-permute-start.16 = (bf16[64,1024]{1,0:T(8,128)(2,1)S(1)}, bf16[64,1024]{1,0:T(8,128)(2,1)S(1)}, u32[]{:S(2)}, u32[]{:S(2)}) collective-permute-start(bf16[64,1024]{1,0:T(8,128)(2,1)S(1)} %get-tuple-element.200), channel_id=1, source_target_pairs={{8,0},{10,2},{12,4},{14,6},{16,8},{18,10},{20,12},{22,14},{24,16},... | collective-permute-start | bytes 393224 | tf_op jit(solution)/shard_map/ppermute | solution.py:15
  232.9 110.5 %collective-permute-start.17 = (bf16[64,1024]{1,0:T(8,128)(2,1)S(1)}, bf16[64,1024]{1,0:T(8,128)(2,1)S(1)}, u32[]{:S(2)}, u32[]{:S(2)}) collective-permute-start(bf16[64,1024]{1,0:T(8,128)(2,1)S(1)} %get-tuple-element.199), channel_id=1, source_target_pairs={{10,0},{12,2},{14,4},{16,6},{18,8},{20,10},{22,12},{24,14},{26,16}... | collective-permute-start | bytes 393224 | tf_op jit(solution)/shard_map/ppermute | solution.py:15
  234.2 109.2 %collective-permute-start.18 = (bf16[64,1024]{1,0:T(8,128)(2,1)S(1)}, bf16[64,1024]{1,0:T(8,128)(2,1)}, u32[]{:S(2)}, u32[]{:S(2)}) collective-permute-start(bf16[64,1024]{1,0:T(8,128)(2,1)S(1)} %get-tuple-element.198), channel_id=1, source_target_pairs={{12,0},{14,2},{16,4},{18,6},{20,8},{22,10},{24,12},{26,14},{28,16}... | collective-permute-start | bytes 393224 | tf_op jit(solution)/shard_map/ppermute | solution.py:15
  (5 other events, 7.4 us)
Sparse Core Ops, SparseCore 0:
  28.3 110.4 all-reduce.3
  218.9 123.0 all-reduce.5
where the time goes:
time: 354 us; the launch traced here: 352 us
  waiting for transfers between devices  219 us (62%)
  starting transfers between devices  39.4 us (11%)
  matrix products  33.9 us (10%)
  local copies, waits for them, and re-layouts  27.3 us (8%)
  other arithmetic  18 us (5%)
  between operations  14.7 us (4%)
    psum x1, waiting for transfers between devices, body(): combined = lax.psum(summary_part, 'ctx')  107 us
    psum x1, waiting for transfers between devices, broadcast(): return lax.psum(jnp.where(mine, array, jnp.zeros_like(array)), axis)  105 us
    ppermute x19, starting transfers between devices, shifted(): return lax.ppermute(block, axis, route)  39.3 us
    dot_general x8, matrix products, head_backward(): lax.dot_general(grad_h, value_h, contract, preferred_element_type=jnp.flo...  9.86 us
    dot_general x8, matrix products, head_backward(): lax.dot_general(probs_round, grad_h, across, preferred_element_type=jnp.f...  9.49 us
    dot_general x8, matrix products, head_backward(): dquery = jnp.dot(dscore, key_h, preferred_element_type=jnp.float32)  7.15 us
  transfers between devices with their start and end apart: 21, of which 4 were waited for; matrix products, arithmetic and copies ran while one was open for 13% of the time, Pallas kernels for 0%

commit v1 on v0

v1 whole, which is shorter than its diff:
```python
import functools

import jax
import jax.numpy as jnp
from jax import lax
from jax.experimental import pallas as pl
from jax.experimental.pallas import tpu as pltpu
from jax.sharding import PartitionSpec as P

BLK = 64
WIN = 7
STRIDE = 16
HEAD_DIM = 128
PLANE = 4
SPAN = PLANE * BLK
PREV = (WIN - 1) * BLK
FAR = PREV - SPAN
OWN = PREV
STRIDED = PREV + SPAN
MESH = pl.DeviceIdType.MESH
LOG2E = 1.4426950408889634


def rows_at(start, size):
    return pl.ds(pl.multiple_of(start, BLK), size)


def columns_at(start, size):
    return pl.ds(pl.multiple_of(start, HEAD_DIM), size)


def kernel(
    n_ctx, n_pp, ticks, group,
    inputs, keys, values, gain, first, head, window, stride,
    grads_out, key_out, value_out,
    xq, gr, kv, res, acc, stage, near_in, far_in, strided_in, total,
    local_sem, plane_send, plane_recv, z_send, z_recv, str_send, str_recv,
    pass_send, pass_recv, res_send, res_recv,
    back_send, back_recv, sback_send, sback_recv, out_send, out_recv,
):
    planes = n_ctx // PLANE
    owners = n_ctx // STRIDE
    step = STRIDE // PLANE
    width = group * HEAD_DIM
    ctx = lax.axis_index("ctx")
    pp = lax.axis_index("pp")
    z = ctx // PLANE
    me = lax.rem(ctx, PLANE)
    last = pp == n_pp - 1

    def at(plane, place):
        return (plane * PLANE + place, pp)

    barrier = pltpu.get_barrier_semaphore()
    for k in range(1, PLANE):
        pl.semaphore_signal(barrier, inc=1, device_id=at(z, lax.rem(me + k, PLANE)), device_id_type=MESH)
    for k in range(1, planes):
        pl.semaphore_signal(barrier, inc=1, device_id=at(lax.rem(z + k, planes), me), device_id_type=MESH)

    @pl.when(pp > 0)
    def _():
        pl.semaphore_signal(barrier, inc=1, device_id=(ctx, pp - 1), device_id_type=MESH)

    @pl.when(pp < n_pp - 1)
    def _():
        pl.semaphore_signal(barrier, inc=1, device_id=(ctx, pp + 1), device_id_type=MESH)

    def pieces(t, place, source):
        cols = columns_at(place * HEAD_DIM, HEAD_DIM)
        wide = columns_at(place * width, width)
        rows = rows_at(source * BLK, BLK)
        own_rows = rows_at(OWN + source * BLK, BLK)
        grads = first if t == 0 else head
        return (
            (keys.at[0, t, :, cols], kv.at[t, 0, own_rows, :]),
            (values.at[0, t, :, cols], kv.at[t, 1, own_rows, :]),
            (inputs.at[0, t, :, wide], xq.at[t, rows, :]),
            (grads.at[0, :, wide] if t == 0 else grads.at[t - 1, :, wide], gr.at[t, rows, :]),
        )

    def local(t, kind):
        src, dst = pieces(t, me, me)[kind]
        return pltpu.make_async_copy(src, dst, local_sem.at[t, kind])

    def remote(t, kind, k):
        place = lax.rem(me + k, PLANE)
        src, dst = pieces(t, place, me)[kind]
        return pltpu.make_async_remote_copy(
            src, dst, plane_send.at[t, kind, k], plane_recv.at[t, kind, me],
            device_id=at(z, place), device_id_type=MESH)

    def arriving(t, kind, k):
        source = lax.rem(me + PLANE - k, PLANE)
        src, dst = pieces(t, me, source)[kind]
        return pltpu.make_async_remote_copy(
            src, dst, plane_send.at[t, kind, k], plane_recv.at[t, kind, source],
            device_id=at(z, source), device_id_type=MESH)

    def exchange(t, kinds, act):
        def run():
            for kind in kinds:
                act(t, kind)
        if t > 0 and kinds == (3,):
            pl.when(last)(run)
        else:
            run()

    def start(t, kind):
        for k in range(1, PLANE):
            remote(t, kind, k).start()

    def start_local(t, kind):
        local(t, kind).start()

    def finish_in(t, kind):
        local(t, kind).wait()
        for k in range(1, PLANE):
            arriving(t, kind, k).wait_recv()

    def finish_out(t, kind):
        for k in range(1, PLANE):
            remote(t, kind, k).wait_send()

    for t in range(ticks):
        exchange(t, (0, 1, 2), start_local)
        exchange(t, (3,), start_local)

    zero = functools.partial(jnp.zeros, dtype=jnp.bfloat16)

    @pl.when(z == 0)
    def _():
        for t in range(ticks):
            kv[t, :, FAR:PREV, :] = zero((2, SPAN, HEAD_DIM))

    @pl.when(z <= 1)
    def _():
        for t in range(ticks):
            kv[t, :, 0:FAR, :] = zero((2, FAR, HEAD_DIM))

    for q in range(owners):
        @pl.when(z <= step * q)
        def _():
            at_row = STRIDED + q * BLK
            for t in range(ticks):
                kv[t, :, at_row:at_row + BLK, :] = zero((2, BLK, HEAD_DIM))

    acc[...] = jnp.zeros_like(acc)

    pl.semaphore_wait(
        barrier,
        PLANE - 1 + planes - 1 + jnp.where(pp > 0, 1, 0) + jnp.where(last, 0, 1))

    for t in range(ticks):
        exchange(t, (0, 1), start)
        exchange(t, (2,), start)
        exchange(t, (3,), start)

    def near(t):
        return pltpu.make_async_remote_copy(
            kv.at[t, :, OWN:OWN + SPAN, :], kv.at[t, :, FAR:PREV, :], z_send.at[t, 0], z_recv.at[t, 0],
            device_id=at(z + 1, me), device_id_type=MESH)

    def far(t):
        return pltpu.make_async_remote_copy(
            kv.at[t, :, OWN + SPAN - FAR:OWN + SPAN, :], kv.at[t, :, 0:FAR, :], z_send.at[t, 1], z_recv.at[t, 1],
            device_id=at(z + 2, me), device_id_type=MESH)

    def strided(t, q, plane):
        return pltpu.make_async_remote_copy(
            kv.at[t, :, OWN:OWN + BLK, :], kv.at[t, :, STRIDED + q * BLK:STRIDED + (q + 1) * BLK, :],
            str_send.at[t, plane], str_recv.at[t, q], device_id=at(plane, me), device_id_type=MESH)

    def each_strided(act):
        for q in range(owners):
            @pl.when(z == step * q)
            def _():
                for plane in range(step * q + 1, planes):
                    act(q, plane)

    def send_keys(t):
        exchange(t, (0, 1), finish_in)
        pl.when(z + 1 < planes)(lambda: near(t).start())
        pl.when(z + 2 < planes)(lambda: far(t).start())
        each_strided(lambda q, plane: strided(t, q, plane).start())

    def take_keys(t):
        pl.when(z >= 1)(lambda: near(t).wait_recv())
        pl.when(z >= 2)(lambda: far(t).wait_recv())
        for q in range(owners):
            pl.when(z > step * q)(lambda: strided(t, q, 0).wait_recv())

    def result_out(t, b):
        return pltpu.make_async_remote_copy(
            res.at[t, rows_at(b * BLK, BLK), :], grads_out.at[0, t, :, columns_at(me * width, width)],
            res_send.at[t, b], res_recv.at[t, me], device_id=at(z, b), device_id_type=MESH)

    def result_in(t, source):
        return pltpu.make_async_remote_copy(
            res.at[t, rows_at(me * BLK, BLK), :], grads_out.at[0, t, :, columns_at(source * width, width)],
            res_send.at[t, me], res_recv.at[t, source], device_id=at(z, source), device_id_type=MESH)

    def result_local(t):
        return pltpu.make_async_copy(
            res.at[t, rows_at(me * BLK, BLK), :], grads_out.at[0, t, :, columns_at(me * width, width)],
            local_sem.at[t, 4])

    def relay(t, b):
        rows = rows_at(b * BLK, BLK)
        return pltpu.make_async_remote_copy(
            res.at[t, rows, :], gr.at[t + 1, rows, :], pass_send.at[t, b], pass_recv.at[t, b],
            device_id=(ctx, jnp.maximum(pp - 1, 0)), device_id_type=MESH)

    def near_back(t):
        return pltpu.make_async_remote_copy(
            stage.at[t, :, FAR:PREV, :], near_in.at[t], back_send.at[t, 0], back_recv.at[t, 0],
            device_id=at(z - 1, me), device_id_type=MESH)

    def far_back(t):
        return pltpu.make_async_remote_copy(
            stage.at[t, :, 0:FAR, :], far_in.at[t], back_send.at[t, 1], back_recv.at[t, 1],
            device_id=at(z - 2, me), device_id_type=MESH)

    def strided_back(t, q, plane):
        return pltpu.make_async_remote_copy(
            stage.at[t, :, STRIDED + q * BLK:STRIDED + (q + 1) * BLK, :], strided_in.at[t, plane],
            sback_send.at[t, q], sback_recv.at[t, plane], device_id=at(step * q, me), device_id_type=MESH)

    my_window = window[0, me]
    my_stride = stride[0, me]
    my_gain = gain[0:1, columns_at(me * width, width)]
    key_count = WIN * BLK + owners * BLK
    row_ids = lax.broadcasted_iota(jnp.int32, (BLK, key_count), 0)
    col_ids = lax.broadcasted_iota(jnp.int32, (BLK, key_count), 1)
    col_block = col_ids // BLK
    is_local = col_block < WIN
    key_offset = col_block - (WIN - 1)
    in_window = key_offset > -my_window
    causal = col_ids <= row_ids + (WIN - 1) * BLK
    strided_block = (col_block - WIN) * STRIDE
    scale = HEAD_DIM ** -0.5
    contract = (((1,), (1,)), ((), ()))
    across = (((0,), (0,)), ((), ()))

    def block_step(t, b):
        block = z * PLANE + b
        key_block = jnp.where(is_local, block + key_offset, strided_block)
        on_stride = (key_block & (my_stride - 1)) == 0
        allowed_local = (key_block >= 0) & causal & (in_window | on_stride)
        allowed_far = on_stride & (key_block <= block - WIN)
        allowed = jnp.where(is_local, jnp.where(allowed_local, 1, 0), jnp.where(allowed_far, 1, 0)) == 1
        rows = slice(b * BLK, (b + 1) * BLK)
        local_rows = slice(b * BLK, (b + WIN) * BLK)
        far_rows = slice(STRIDED, STRIDED + owners * BLK)
        key_b = jnp.concatenate([kv[t, 0, local_rows, :], kv[t, 0, far_rows, :]], axis=0)
        value_b = jnp.concatenate([kv[t, 1, local_rows, :], kv[t, 1, far_rows, :]], axis=0)
        queries = (xq[t, rows, :].astype(jnp.float32) * my_gain).astype(jnp.bfloat16)
        grad = gr[t, rows, :]

        def stack(matrix):
            return jnp.concatenate([matrix[:, h * HEAD_DIM:(h + 1) * HEAD_DIM] for h in range(group)], axis=0)

        query_b, grad_b = stack(queries), stack(grad)
        scores = lax.dot_general(query_b, key_b, contract, preferred_element_type=jnp.float32)
        scores = scores.reshape(group, BLK, key_count)
        scores = jnp.where(allowed[None], scores, jnp.float32(-1e30))
        peak = jnp.max(scores, axis=2, keepdims=True)
        weights = jnp.exp2((scores - peak) * jnp.float32(scale * LOG2E))
        probs = weights * (1.0 / jnp.sum(weights, axis=2, keepdims=True))
        grad_prob = lax.dot_general(grad_b, value_b, contract, preferred_element_type=jnp.float32)
        grad_prob = grad_prob.reshape(group, BLK, key_count)
        delta = jnp.sum(probs * grad_prob, axis=2, keepdims=True)
        dscore = (probs * (grad_prob - delta) * jnp.float32(scale)).astype(jnp.bfloat16)
        dscore = dscore.reshape(group * BLK, key_count)
        probs = probs.astype(jnp.bfloat16).reshape(group * BLK, key_count)
        dquery = jnp.dot(dscore, key_b, preferred_element_type=jnp.float32)
        dquery = jnp.concatenate([dquery[h * BLK:(h + 1) * BLK] for h in range(group)], axis=1)
        res[t, rows, :] = (grad.astype(jnp.float32) + my_gain * dquery).astype(jnp.bfloat16)
        for part, term in enumerate((
            lax.dot_general(dscore, query_b, across, preferred_element_type=jnp.float32),
            lax.dot_general(probs, grad_b, across, preferred_element_type=jnp.float32),
        )):
            acc[t, part, local_rows, :] += term[:WIN * BLK]
            acc[t, part, far_rows, :] += term[WIN * BLK:]

    for t in range(ticks):
        send_keys(t)
    for t in range(ticks):
        exchange(t, (2,), finish_in)
        if t == 0:
            finish_in(t, 3)
        else:
            pl.when(last)(lambda: finish_in(t, 3))

            @pl.when(pp < n_pp - 1)
            def _():
                for b in range(PLANE):
                    relay(t - 1, b).wait_recv()
        take_keys(t)
        for b in range(PLANE):
            block_step(t, b)
            if t + 1 < ticks:
                pl.when(pp > 0)(lambda: relay(t, b).start())
            pl.when(me != b)(lambda: result_out(t, b).start())
            if b * BLK + BLK == FAR:
                stage[t, :, 0:FAR, :] = acc[t, :, 0:FAR, :].astype(jnp.bfloat16)
                pl.when(z >= 2)(lambda: far_back(t).start())
        result_local(t).start()
        stage[t, :, FAR:PREV, :] = acc[t, :, FAR:PREV, :].astype(jnp.bfloat16)
        pl.when(z >= 1)(lambda: near_back(t).start())
        stage[t, :, STRIDED:, :] = acc[t, :, STRIDED:, :].astype(jnp.bfloat16)
        for q in range(owners):
            pl.when(z > step * q)(lambda: strided_back(t, q, z).start())

    outs = (key_out, value_out)

    def total_out(t, part, k):
        b = lax.rem(me + k, PLANE)
        return pltpu.make_async_remote_copy(
            total.at[t, part, rows_at(b * BLK, BLK), :],
            outs[part].at[0, t, :, columns_at(me * HEAD_DIM, HEAD_DIM)],
            out_send.at[t, part, k], out_recv.at[t, part, me], device_id=at(z, b), device_id_type=MESH)

    def total_in(t, part, k):
        source = lax.rem(me + PLANE - k, PLANE)
        return pltpu.make_async_remote_copy(
            total.at[t, part, rows_at(me * BLK, BLK), :],
            outs[part].at[0, t, :, columns_at(source * HEAD_DIM, HEAD_DIM)],
            out_send.at[t, part, k], out_recv.at[t, part, source], device_id=at(z, source), device_id_type=MESH)

    def total_local(t, part):
        return pltpu.make_async_copy(
            total.at[t, part, rows_at(me * BLK, BLK), :],
            outs[part].at[0, t, :, columns_at(me * HEAD_DIM, HEAD_DIM)], local_sem.at[t, 5 + part])

    for t in range(ticks):
        @pl.when(z + 1 < planes)
        def _():
            near_back(t).wait_recv()
            acc[t, :, OWN:OWN + SPAN, :] += near_in[t].astype(jnp.float32)

        @pl.when(z + 2 < planes)
        def _():
            far_back(t).wait_recv()
            acc[t, :, OWN + SPAN - FAR:OWN + SPAN, :] += far_in[t].astype(jnp.float32)

        def add_strided(q, plane):
            strided_back(t, q, plane).wait_recv()
            acc[t, :, OWN:OWN + BLK, :] += strided_in[t, plane].astype(jnp.float32)

        each_strided(add_strided)
        total[t] = acc[t, :, OWN:OWN + SPAN, :].astype(jnp.bfloat16)
        for part in range(2):
            for k in range(1, PLANE):
                total_out(t, part, k).start()
            total_local(t, part).start()

    for t in range(ticks):
        exchange(t, (0, 1, 2), finish_out)
        exchange(t, (3,), finish_out)
        pl.when(z + 1 < planes)(lambda: near(t).wait_send())
        pl.when(z + 2 < planes)(lambda: far(t).wait_send())
        each_strided(lambda q, plane: strided(t, q, plane).wait_send())
        for b in range(PLANE):
            if t + 1 < ticks:
                pl.when(pp > 0)(lambda: relay(t, b).wait_send())
            pl.when(me != b)(lambda: result_out(t, b).wait_send())
        pl.when(z >= 2)(lambda: far_back(t).wait_send())
        pl.when(z >= 1)(lambda: near_back(t).wait_send())
        for q in range(owners):
            pl.when(z > step * q)(lambda: strided_back(t, q, z).wait_send())
        result_local(t).wait()
        for k in range(1, PLANE):
            result_in(t, lax.rem(me + k, PLANE)).wait_recv()
        for part in range(2):
            total_local(t, part).wait()
            for k in range(1, PLANE):
                total_out(t, part, k).wait_send()
                total_in(t, part, k).wait_recv()


def body(n_ctx, n_pp, inputs, keys, values, gain, first, head, window, stride):
    ticks = inputs.shape[1]
    feat = inputs.shape[-1]
    kv_heads = keys.shape[-1] // HEAD_DIM
    group = feat // (kv_heads * HEAD_DIM)
    planes = n_ctx // PLANE
    owners = n_ctx // STRIDE
    rows = STRIDED + owners * BLK
    width = group * HEAD_DIM
    bf16, f32 = jnp.bfloat16, jnp.float32
    dma = pltpu.SemaphoreType.DMA
    anywhere = pl.BlockSpec(memory_space=pl.ANY)
    scalars = pl.BlockSpec(memory_space=pltpu.SMEM)
    return pl.pallas_call(
        functools.partial(kernel, n_ctx, n_pp, ticks, group),
        out_shape=[jax.ShapeDtypeStruct(a.shape, bf16) for a in (inputs, keys, values)],
        in_specs=[anywhere] * 3 + [pl.BlockSpec(memory_space=pltpu.VMEM)] + [anywhere] * 2 + [scalars] * 2,
        out_specs=[anywhere] * 3,
        scratch_shapes=[
            pltpu.VMEM((ticks, SPAN, width), bf16),
            pltpu.VMEM((ticks, SPAN, width), bf16),
            pltpu.VMEM((ticks, 2, rows, HEAD_DIM), bf16),
            pltpu.VMEM((ticks, SPAN, width), bf16),
            pltpu.VMEM((ticks, 2, rows, HEAD_DIM), f32),
            pltpu.VMEM((ticks, 2, rows, HEAD_DIM), bf16),
            pltpu.VMEM((ticks, 2, SPAN, HEAD_DIM), bf16),
            pltpu.VMEM((ticks, 2, FAR, HEAD_DIM), bf16),
            pltpu.VMEM((ticks, planes, 2, BLK, HEAD_DIM), bf16),
            pltpu.VMEM((ticks, 2, SPAN, HEAD_DIM), bf16),
            dma((ticks, 7)),
            dma((ticks, 4, PLANE)), dma((ticks, 4, PLANE)),
            dma((ticks, 2)), dma((ticks, 2)),
            dma((ticks, planes)), dma((ticks, owners)),
            dma((ticks, PLANE)), dma((ticks, PLANE)),
            dma((ticks, PLANE)), dma((ticks, PLANE)),
            dma((ticks, 2)), dma((ticks, 2)),
            dma((ticks, owners)), dma((ticks, planes)),
            dma((ticks, 2, PLANE)), dma((ticks, 2, PLANE)),
        ],
        compiler_params=pltpu.CompilerParams(
            collective_id=0, has_side_effects=True, vmem_limit_bytes=40 * 1024 * 1024),
        name="plane_backward",
    )(inputs, keys, values, gain, first, head, window, stride)


def solution(mesh):
    in_specs = (
        P("pp", None, "ctx", None),
        P("pp", None, "ctx", None),
        P("pp", None, "ctx", None),
        P("pp", None),
        P("pp", "ctx", None),
        P(None, "ctx", None),
        P("pp", None),
        P("pp", None),
    )
    out_specs = (P("pp", None, "ctx", None), P("pp", None, "ctx", None), P("pp", None, "ctx", None))
    run = functools.partial(body, mesh.shape["ctx"], mesh.shape["pp"])
    return jax.shard_map(run, mesh=mesh, in_specs=in_specs, out_specs=out_specs, check_vma=False)
```

time: 354 us -> 48.2 us (0.14)
  waiting for transfers between devices: 219 us -> 0 us
  starting transfers between devices: 39.4 us -> 0 us
  Pallas kernels: 0 us -> 38.4 us
  matrix products: 33.9 us -> 0 us
  local copies, waits for them, and re-layouts: 27.3 us -> 8.85 us
  other arithmetic: 18 us -> 0 us
  between operations: 14.7 us -> 0.66 us
    psum x2 -> x0, waiting for transfers between devices: 212 us -> none  [the longest x1 107 us: body(): combined = lax.psum(summary_part, 'ctx')]
    ppermute x19 -> x0, starting transfers between devices: 39.3 us -> none  [shifted(): return lax.ppermute(block, axis, route)]
    pallas_call x0 -> x1, Pallas kernels: none -> 38.4 us  [body(): pl.pallas_call(functools.partial(kernel, n_ctx, n_pp, ticks, group), out_...]
    dot_general x40 -> x0, matrix products: 33.9 us -> none  [the longest x8 9.86 us: head_backward(): lax.dot_general(grad_h, value_h, contract, preferred_element_type=jnp.flo...]
    reshape x8 -> x0, local copies, waits for them, and re-layouts: 6.96 us -> none  [the longest x2 3.12 us: local_backward(): dquery.reshape(kv_heads, group_size, rows, HEAD_DIM).transpose(2, 0, 1, 3)]
    ppermute x19 -> x0, waiting for transfers between devices: 6.83 us -> none  [shifted(): return lax.ppermute(block, axis, route)]
    slice x7 -> x0, local copies, waits for them, and re-layouts: 5.62 us -> none  [the longest x2 3.06 us: local_backward(): kv_all[:, kv_width:].reshape(key_count, kv_heads, HEAD_DIM)]
    another operation x24 -> x0, local copies, waits for them, and re-layouts: 5.14 us -> none
  transfers between devices with their start and end apart: 21 -> 0, of which waited for: 4 -> 0; matrix products, arithmetic and copies ran while one was open for 13% -> 0% of each run, Pallas kernels for 0% -> 0%
where the time goes in v1:
time: 48.2 us; the launch traced here: 47.9 us
  Pallas kernels  38.4 us (80%)
  local copies, waits for them, and re-layouts  8.85 us (18%)
  between operations  0.66 us (1%)
    pallas_call x1, Pallas kernels, body(): pl.pallas_call(functools.partial(kernel, n_ctx, n_pp, ticks, group), out_...  38.4 us
    unnamed x19, local copies, waits for them, and re-layouts  8.85 us

profile of v1, /device:TPU:0, one launch (start us, length us, event | category | flops | bytes accessed | tf_op | source)
XLA Modules:
  0.0 47.9 jit_solution(4440997870218577726)
XLA Ops:
  0.6 0.0 copy-start
  0.6 1.0 %copy-done = bf16[1,2,64,2048]{3,2,1,0:T(8,128)(2,1)S(1)} copy-done((bf16[1,2,64,2048]{3,2,1,0:T(8,128)(2,1)S(1)}, bf16[1,2,64,2048]{3,2,1,0:T(8,128)(2,1)}, u32[]{:S(2)}) %copy-start) | copy-done | bytes 524312
  1.7 0.0 copy-start.1
  1.7 0.9 %copy-done.1 = bf16[1,64,2048]{2,1,0:T(8,128)(2,1)S(1)} copy-done((bf16[1,64,2048]{2,1,0:T(8,128)(2,1)S(1)}, bf16[1,64,2048]{2,1,0:T(8,128)(2,1)}, u32[]{:S(2)}) %copy-start.1) | copy-done | bytes 262168
  2.6 0.0 copy-start.2
  2.6 0.9 %copy-done.2 = bf16[1,64,2048]{2,1,0:T(8,128)(2,1)S(1)} copy-done((bf16[1,64,2048]{2,1,0:T(8,128)(2,1)S(1)}, bf16[1,64,2048]{2,1,0:T(8,128)(2,1)}, u32[]{:S(2)}) %copy-start.2) | copy-done | bytes 262168
  3.6 0.0 copy-start.3
  3.6 0.9 %copy-done.3 = bf16[1,2,64,512]{3,2,1,0:T(8,128)(2,1)S(1)} copy-done((bf16[1,2,64,512]{3,2,1,0:T(8,128)(2,1)S(1)}, bf16[1,2,64,512]{3,2,1,0:T(8,128)(2,1)}, u32[]{:S(2)}) %copy-start.3) | copy-done | bytes 131096
  4.5 0.0 copy-start.4
  4.5 0.9 %copy-done.4 = bf16[1,2,64,512]{3,2,1,0:T(8,128)(2,1)S(1)} copy-done((bf16[1,2,64,512]{3,2,1,0:T(8,128)(2,1)S(1)}, bf16[1,2,64,512]{3,2,1,0:T(8,128)(2,1)}, u32[]{:S(2)}) %copy-start.4) | copy-done | bytes 131096
  5.4 0.0 copy-start.5
  5.4 0.7 %copy-done.5 = f32[1,2048]{1,0:T(1,128)S(1)} copy-done((f32[1,2048]{1,0:T(1,128)S(1)}, f32[1,2048]{1,0:T(1,128)}, u32[]{:S(2)}) %copy-start.5) | copy-done | bytes 8216
  6.1 0.0 copy-start.6
  6.1 0.7 %copy-done.6 = s32[1,4]{1,0:T(1,128)S(1)} copy-done((s32[1,4]{1,0:T(1,128)S(1)}, s32[1,4]{1,0:T(1,128)}, u32[]{:S(2)}) %copy-start.6) | copy-done | bytes 40
  6.7 0.0 copy-start.7
  6.7 0.7 %copy-done.7 = s32[1,4]{1,0:T(1,128)S(1)} copy-done((s32[1,4]{1,0:T(1,128)S(1)}, s32[1,4]{1,0:T(1,128)}, u32[]{:S(2)}) %copy-start.7) | copy-done | bytes 40
  7.4 38.4 %plane_backward.1 = (bf16[1,2,64,2048]{3,2,1,0:T(8,128)(2,1)S(1)}, bf16[1,2,64,512]{3,2,1,0:T(8,128)(2,1)S(1)}, bf16[1,2,64,512]{3,2,1,0:T(8,128)(2,1)S(1)}) custom-call(bf16[1,2,64,2048]{3,2,1,0:T(8,128)(2,1)S(1)} %copy-done, bf16[1,2,64,512]{3,2,1,0:T(8,128)(2,1)S(1)} %copy-done.3, bf16[1,2,64,512]{3,2,1,0:T(8,128)(2,1)S(1)} %copy-done.4, ...), custom_call_target="tpu_custom_call" | custom-call | tf_op jit(solution)/shard_map/plane_backward/pallas_call | solution.py:394
  45.8 0.8 %copy.14 = bf16[1,2,64,2048]{3,2,1,0:T(8,128)(2,1)} copy(bf16[1,2,64,2048]{3,2,1,0:T(8,128)(2,1)S(1)} %get-tuple-element.6) | data formatting | bytes 1048576
  46.6 0.7 %copy.15 = bf16[1,2,64,512]{3,2,1,0:T(8,128)(2,1)} copy(bf16[1,2,64,512]{3,2,1,0:T(8,128)(2,1)S(1)} %get-tuple-element.7) | data formatting | bytes 262144
  47.2 0.7 %copy.16 = bf16[1,2,64,512]{3,2,1,0:T(8,128)(2,1)} copy(bf16[1,2,64,512]{3,2,1,0:T(8,128)(2,1)S(1)} %get-tuple-element.8) | data formatting | bytes 262144
Async XLA Ops:
  0.6 1.0 %copy-start = (bf16[1,2,64,2048]{3,2,1,0:T(8,128)(2,1)S(1)}, bf16[1,2,64,2048]{3,2,1,0:T(8,128)(2,1)}, u32[]{:S(2)}) copy-start(bf16[1,2,64,2048]{3,2,1,0:T(8,128)(2,1)} %inputs.1) | copy-start | bytes 1572868
  1.7 0.9 %copy-start.1 = (bf16[1,64,2048]{2,1,0:T(8,128)(2,1)S(1)}, bf16[1,64,2048]{2,1,0:T(8,128)(2,1)}, u32[]{:S(2)}) copy-start(bf16[1,64,2048]{2,1,0:T(8,128)(2,1)} %first.1) | copy-start | bytes 786436
  2.6 0.9 %copy-start.2 = (bf16[1,64,2048]{2,1,0:T(8,128)(2,1)S(1)}, bf16[1,64,2048]{2,1,0:T(8,128)(2,1)}, u32[]{:S(2)}) copy-start(bf16[1,64,2048]{2,1,0:T(8,128)(2,1)} %head.1) | copy-start | bytes 786436
  3.6 0.9 %copy-start.3 = (bf16[1,2,64,512]{3,2,1,0:T(8,128)(2,1)S(1)}, bf16[1,2,64,512]{3,2,1,0:T(8,128)(2,1)}, u32[]{:S(2)}) copy-start(bf16[1,2,64,512]{3,2,1,0:T(8,128)(2,1)} %keys.1) | copy-start | bytes 393220
  4.5 0.9 %copy-start.4 = (bf16[1,2,64,512]{3,2,1,0:T(8,128)(2,1)S(1)}, bf16[1,2,64,512]{3,2,1,0:T(8,128)(2,1)}, u32[]{:S(2)}) copy-start(bf16[1,2,64,512]{3,2,1,0:T(8,128)(2,1)} %values.1) | copy-start | bytes 393220
  5.4 0.7 %copy-start.5 = (f32[1,2048]{1,0:T(1,128)S(1)}, f32[1,2048]{1,0:T(1,128)}, u32[]{:S(2)}) copy-start(f32[1,2048]{1,0:T(1,128)} %gain.1) | copy-start | bytes 24580
  6.1 0.7 %copy-start.6 = (s32[1,4]{1,0:T(1,128)S(1)}, s32[1,4]{1,0:T(1,128)}, u32[]{:S(2)}) copy-start(s32[1,4]{1,0:T(1,128)} %window.1) | copy-start | bytes 52
  6.7 0.7 %copy-start.7 = (s32[1,4]{1,0:T(1,128)S(1)}, s32[1,4]{1,0:T(1,128)}, u32[]{:S(2)}) copy-start(s32[1,4]{1,0:T(1,128)} %stride.1) | copy-start | bytes 52

commit v2 on v1

--- a/solution.py
+++ b/solution.py
@@ -31,9 +31,9 @@
 
 def kernel(
     n_ctx, n_pp, ticks, group,
-    inputs, keys, values, gain, first, head, window, stride,
+    inputs, keys, values, gain_hbm, first, head, window_hbm, stride_hbm,
     grads_out, key_out, value_out,
-    xq, gr, kv, res, acc, stage, near_in, far_in, strided_in, total,
+    xq, gr, kv, res, acc, stage, near_in, far_in, strided_in, total, gain, window, stride, small_sem,
     local_sem, plane_send, plane_recv, z_send, z_recv, str_send, str_recv,
     pass_send, pass_recv, res_send, res_recv,
     back_send, back_recv, sback_send, sback_recv, out_send, out_recv,
@@ -121,6 +121,12 @@
         for k in range(1, PLANE):
             remote(t, kind, k).wait_send()
 
+    small = [
+        pltpu.make_async_copy(src, dst, small_sem.at[i])
+        for i, (src, dst) in enumerate(((gain_hbm, gain), (window_hbm, window), (stride_hbm, stride)))
+    ]
+    for copy in small:
+        copy.start()
     for t in range(ticks):
         exchange(t, (0, 1, 2), start_local)
         exchange(t, (3,), start_local)
@@ -225,29 +231,34 @@
             stage.at[t, :, STRIDED + q * BLK:STRIDED + (q + 1) * BLK, :], strided_in.at[t, plane],
             sback_send.at[t, q], sback_recv.at[t, plane], device_id=at(step * q, me), device_id_type=MESH)
 
+    for copy in small:
+        copy.wait()
     my_window = window[0, me]
     my_stride = stride[0, me]
     my_gain = gain[0:1, columns_at(me * width, width)]
-    key_count = WIN * BLK + owners * BLK
-    row_ids = lax.broadcasted_iota(jnp.int32, (BLK, key_count), 0)
-    col_ids = lax.broadcasted_iota(jnp.int32, (BLK, key_count), 1)
-    col_block = col_ids // BLK
-    is_local = col_block < WIN
-    key_offset = col_block - (WIN - 1)
-    in_window = key_offset > -my_window
-    causal = col_ids <= row_ids + (WIN - 1) * BLK
-    strided_block = (col_block - WIN) * STRIDE
+    key_ids = lax.broadcasted_iota(jnp.int32, (BLK, group * BLK), 0)
+    query_ids = lax.broadcasted_iota(jnp.int32, (BLK, group * BLK), 1) % BLK
+    causal = jnp.where(key_ids <= query_ids, jnp.float32(0), jnp.float32(-1e30))
     scale = HEAD_DIM ** -0.5
     contract = (((1,), (1,)), ((), ()))
-    across = (((0,), (0,)), ((), ()))
+    rows_of = lambda matrix, c: matrix[c * BLK:(c + 1) * BLK]
+
+    def bias(block, c):
+        if c < WIN:
+            distance = WIN - 1 - c
+            key_block = block - distance
+            near_enough = jnp.where(distance < my_window, 1, 0)
+            on_stride = jnp.where((key_block & (my_stride - 1)) == 0, 1, 0)
+            inside = jnp.where(key_block >= 0, 1, 0)
+            allowed = inside * jnp.maximum(near_enough, on_stride)
+        else:
+            key_block = (c - WIN) * STRIDE
+            on_stride = jnp.where((key_block & (my_stride - 1)) == 0, 1, 0)
+            allowed = on_stride * jnp.where(key_block <= block - WIN, 1, 0)
+        return jnp.where(allowed == 1, jnp.float32(0), jnp.float32(-1e30))
 
     def block_step(t, b):
         block = z * PLANE + b
-        key_block = jnp.where(is_local, block + key_offset, strided_block)
-        on_stride = (key_block & (my_stride - 1)) == 0
-        allowed_local = (key_block >= 0) & causal & (in_window | on_stride)
-        allowed_far = on_stride & (key_block <= block - WIN)
-        allowed = jnp.where(is_local, jnp.where(allowed_local, 1, 0), jnp.where(allowed_far, 1, 0)) == 1
         rows = slice(b * BLK, (b + 1) * BLK)
         local_rows = slice(b * BLK, (b + WIN) * BLK)
         far_rows = slice(STRIDED, STRIDED + owners * BLK)
@@ -260,30 +271,71 @@
             return jnp.concatenate([matrix[:, h * HEAD_DIM:(h + 1) * HEAD_DIM] for h in range(group)], axis=0)
 
         query_b, grad_b = stack(queries), stack(grad)
-        scores = lax.dot_general(query_b, key_b, contract, preferred_element_type=jnp.float32)
-        scores = scores.reshape(group, BLK, key_count)
-        scores = jnp.where(allowed[None], scores, jnp.float32(-1e30))
-        peak = jnp.max(scores, axis=2, keepdims=True)
+        scores = lax.dot_general(key_b, query_b, contract, preferred_element_type=jnp.float32)
+        scores = jnp.concatenate(
+            [rows_of(scores, c) + (causal if c == WIN - 1 else bias(block, c)) for c in range(WIN + owners)], axis=0)
+        peak = jnp.max(scores, axis=0, keepdims=True)
         weights = jnp.exp2((scores - peak) * jnp.float32(scale * LOG2E))
-        probs = weights * (1.0 / jnp.sum(weights, axis=2, keepdims=True))
-        grad_prob = lax.dot_general(grad_b, value_b, contract, preferred_element_type=jnp.float32)
-        grad_prob = grad_prob.reshape(group, BLK, key_count)
-        delta = jnp.sum(probs * grad_prob, axis=2, keepdims=True)
+        inverse = 1.0 / jnp.sum(weights, axis=0, keepdims=True)
+        grad_prob = lax.dot_general(value_b, grad_b, contract, preferred_element_type=jnp.float32)
+        probs = weights * inverse
+        delta = jnp.sum(probs * grad_prob, axis=0, keepdims=True)
         dscore = (probs * (grad_prob - delta) * jnp.float32(scale)).astype(jnp.bfloat16)
-        dscore = dscore.reshape(group * BLK, key_count)
-        probs = probs.astype(jnp.bfloat16).reshape(group * BLK, key_count)
-        dquery = jnp.dot(dscore, key_b, preferred_element_type=jnp.float32)
-        dquery = jnp.concatenate([dquery[h * BLK:(h + 1) * BLK] for h in range(group)], axis=1)
+        probs = probs.astype(jnp.bfloat16)
+        dquery = jnp.dot(key_b.T, dscore, preferred_element_type=jnp.float32).T
+        dquery = jnp.concatenate([rows_of(dquery, h) for h in range(group)], axis=1)
         res[t, rows, :] = (grad.astype(jnp.float32) + my_gain * dquery).astype(jnp.bfloat16)
         for part, term in enumerate((
-            lax.dot_general(dscore, query_b, across, preferred_element_type=jnp.float32),
-            lax.dot_general(probs, grad_b, across, preferred_element_type=jnp.float32),
+            jnp.dot(dscore, query_b, preferred_element_type=jnp.float32),
+            jnp.dot(probs, grad_b, preferred_element_type=jnp.float32),
         )):
             acc[t, part, local_rows, :] += term[:WIN * BLK]
             acc[t, part, far_rows, :] += term[WIN * BLK:]
 
-    for t in range(ticks):
-        send_keys(t)
+    outs = (key_out, value_out)
+
+    def total_out(t, part, k):
+        b = lax.rem(me + k, PLANE)
+        return pltpu.make_async_remote_copy(
+            total.at[t, part, rows_at(b * BLK, BLK), :],
+            outs[part].at[0, t, :, columns_at(me * HEAD_DIM, HEAD_DIM)],
+            out_send.at[t, part, k], out_recv.at[t, part, me], device_id=at(z, b), device_id_type=MESH)
+
+    def total_in(t, part, k):
+        source = lax.rem(me + PLANE - k, PLANE)
+        return pltpu.make_async_remote_copy(
+            total.at[t, part, rows_at(me * BLK, BLK), :],
+            outs[part].at[0, t, :, columns_at(source * HEAD_DIM, HEAD_DIM)],
+            out_send.at[t, part, k], out_recv.at[t, part, source], device_id=at(z, source), device_id_type=MESH)
+
+    def total_local(t, part):
+        return pltpu.make_async_copy(
+            total.at[t, part, rows_at(me * BLK, BLK), :],
+            outs[part].at[0, t, :, columns_at(me * HEAD_DIM, HEAD_DIM)], local_sem.at[t, 5 + part])
+
+    def finish(t):
+        @pl.when(z + 1 < planes)
+        def _():
+            near_back(t).wait_recv()
+            acc[t, :, OWN:OWN + SPAN, :] += near_in[t].astype(jnp.float32)
+
+        @pl.when(z + 2 < planes)
+        def _():
+            far_back(t).wait_recv()
+            acc[t, :, OWN + SPAN - FAR:OWN + SPAN, :] += far_in[t].astype(jnp.float32)
+
+        def add_strided(q, plane):
+            strided_back(t, q, plane).wait_recv()
+            acc[t, :, OWN:OWN + BLK, :] += strided_in[t, plane].astype(jnp.float32)
+
+        each_strided(add_strided)
+        total[t] = acc[t, :, OWN:OWN + SPAN, :].astype(jnp.bfloat16)
+        for part in range(2):
+            for k in range(1, PLANE):
+                total_out(t, part, k).start()
+            total_local(t, part).start()
+
+    send_keys(0)
     for t in range(ticks):
         exchange(t, (2,), finish_in)
         if t == 0:
@@ -298,12 +350,16 @@
         take_keys(t)
         for b in range(PLANE):
             block_step(t, b)
+            if b == 0 and t + 1 < ticks:
+                send_keys(t + 1)
             if t + 1 < ticks:
                 pl.when(pp > 0)(lambda: relay(t, b).start())
             pl.when(me != b)(lambda: result_out(t, b).start())
             if b * BLK + BLK == FAR:
                 stage[t, :, 0:FAR, :] = acc[t, :, 0:FAR, :].astype(jnp.bfloat16)
                 pl.when(z >= 2)(lambda: far_back(t).start())
+            if t > 0 and b == PLANE - 2:
+                finish(t - 1)
         result_local(t).start()
         stage[t, :, FAR:PREV, :] = acc[t, :, FAR:PREV, :].astype(jnp.bfloat16)
         pl.when(z >= 1)(lambda: near_back(t).start())
@@ -311,48 +367,7 @@
         for q in range(owners):
             pl.when(z > step * q)(lambda: strided_back(t, q, z).start())
 
-    outs = (key_out, value_out)
-
-    def total_out(t, part, k):
-        b = lax.rem(me + k, PLANE)
-        return pltpu.make_async_remote_copy(
-            total.at[t, part, rows_at(b * BLK, BLK), :],
-            outs[part].at[0, t, :, columns_at(me * HEAD_DIM, HEAD_DIM)],
-            out_send.at[t, part, k], out_recv.at[t, part, me], device_id=at(z, b), device_id_type=MESH)
-
-    def total_in(t, part, k):
-        source = lax.rem(me + PLANE - k, PLANE)
-        return pltpu.make_async_remote_copy(
-            total.at[t, part, rows_at(me * BLK, BLK), :],
-            outs[part].at[0, t, :, columns_at(source * HEAD_DIM, HEAD_DIM)],
-            out_send.at[t, part, k], out_recv.at[t, part, source], device_id=at(z, source), device_id_type=MESH)
-
-    def total_local(t, part):
-        return pltpu.make_async_copy(
-            total.at[t, part, rows_at(me * BLK, BLK), :],
-            outs[part].at[0, t, :, columns_at(me * HEAD_DIM, HEAD_DIM)], local_sem.at[t, 5 + part])
-
-    for t in range(ticks):
-        @pl.when(z + 1 < planes)
-        def _():
-            near_back(t).wait_recv()
-            acc[t, :, OWN:OWN + SPAN, :] += near_in[t].astype(jnp.float32)
-
-        @pl.when(z + 2 < planes)
-        def _():
-            far_back(t).wait_recv()
-            acc[t, :, OWN + SPAN - FAR:OWN + SPAN, :] += far_in[t].astype(jnp.float32)
-
-        def add_strided(q, plane):
-            strided_back(t, q, plane).wait_recv()
-            acc[t, :, OWN:OWN + BLK, :] += strided_in[t, plane].astype(jnp.float32)
-
-        each_strided(add_strided)
-        total[t] = acc[t, :, OWN:OWN + SPAN, :].astype(jnp.bfloat16)
-        for part in range(2):
-            for k in range(1, PLANE):
-                total_out(t, part, k).start()
-            total_local(t, part).start()
+    finish(ticks - 1)
 
     for t in range(ticks):
         exchange(t, (0, 1, 2), finish_out)
@@ -378,6 +393,17 @@
                 total_in(t, part, k).wait_recv()
 
 
+def hand_out(a, b, c, a_out, b_out, c_out, sem):
+    copies = [
+        pltpu.make_async_copy(src, dst, sem.at[i])
+        for i, (src, dst) in enumerate(((a, a_out), (b, b_out), (c, c_out)))
+    ]
+    for copy in copies:
+        copy.start()
+    for copy in copies:
+        copy.wait()
+
+
 def body(n_ctx, n_pp, inputs, keys, values, gain, first, head, window, stride):
     ticks = inputs.shape[1]
     feat = inputs.shape[-1]
@@ -390,11 +416,10 @@
     bf16, f32 = jnp.bfloat16, jnp.float32
     dma = pltpu.SemaphoreType.DMA
     anywhere = pl.BlockSpec(memory_space=pl.ANY)
-    scalars = pl.BlockSpec(memory_space=pltpu.SMEM)
-    return pl.pallas_call(
+    outs = pl.pallas_call(
         functools.partial(kernel, n_ctx, n_pp, ticks, group),
         out_shape=[jax.ShapeDtypeStruct(a.shape, bf16) for a in (inputs, keys, values)],
-        in_specs=[anywhere] * 3 + [pl.BlockSpec(memory_space=pltpu.VMEM)] + [anywhere] * 2 + [scalars] * 2,
+        in_specs=[pl.BlockSpec(memory_space=pltpu.HBM)] * 8,
         out_specs=[anywhere] * 3,
         scratch_shapes=[
             pltpu.VMEM((ticks, SPAN, width), bf16),
@@ -407,6 +432,8 @@
             pltpu.VMEM((ticks, 2, FAR, HEAD_DIM), bf16),
             pltpu.VMEM((ticks, planes, 2, BLK, HEAD_DIM), bf16),
             pltpu.VMEM((ticks, 2, SPAN, HEAD_DIM), bf16),
+            pltpu.VMEM(gain.shape, f32), pltpu.SMEM(window.shape, jnp.int32), pltpu.SMEM(stride.shape, jnp.int32),
+            dma((3,)),
             dma((ticks, 7)),
             dma((ticks, 4, PLANE)), dma((ticks, 4, PLANE)),
             dma((ticks, 2)), dma((ticks, 2)),
@@ -418,9 +445,18 @@
             dma((ticks, 2, PLANE)), dma((ticks, 2, PLANE)),
         ],
         compiler_params=pltpu.CompilerParams(
-            collective_id=0, has_side_effects=True, vmem_limit_bytes=40 * 1024 * 1024),
+            collective_id=0, has_side_effects=True, vmem_limit_bytes=64 * 1024 * 1024),
         name="plane_backward",
     )(inputs, keys, values, gain, first, head, window, stride)
+    return pl.pallas_call(
+        hand_out,
+        out_shape=[jax.ShapeDtypeStruct(a.shape, bf16) for a in (inputs, keys, values)],
+        in_specs=[anywhere] * 3,
+        out_specs=[pl.BlockSpec(memory_space=pltpu.HBM)] * 3,
+        scratch_shapes=[dma((3,))],
+        compiler_params=pltpu.CompilerParams(vmem_limit_bytes=64 * 1024 * 1024),
+        name="hand_out",
+    )(*outs)
 
 
 def solution(mesh):

time: 48.2 us -> 64.1 us (1.33)
  Pallas kernels: 38.4 us -> 63.3 us
  local copies, waits for them, and re-layouts: 8.85 us -> 0 us
    pallas_call x0 -> x1, Pallas kernels: none -> 25 us  [body(): pl.pallas_call(hand_out, out_shape=[jax.ShapeDtypeStruct(a.shape, bf16) f...]
    unnamed x19 -> x0, local copies, waits for them, and re-layouts: 8.85 us -> none
where the time goes in v2:
time: 64.1 us; the launch traced here: 64 us
  Pallas kernels  63.3 us (99%)
    pallas_call x1, Pallas kernels, body(): pl.pallas_call(functools.partial(kernel, n_ctx, n_pp, ticks, group), out_...  38.4 us
    pallas_call x1, Pallas kernels, body(): pl.pallas_call(hand_out, out_shape=[jax.ShapeDtypeStruct(a.shape, bf16) f...  25 us

profile of v2, /device:TPU:0, one launch (start us, length us, event | category | flops | bytes accessed | tf_op | source)
XLA Modules:
  0.0 64.0 jit_solution(17994081028206255293)
XLA Ops:
  0.6 38.4 %plane_backward.1 = (bf16[1,2,64,2048]{3,2,1,0:T(8,128)(2,1)}, bf16[1,2,64,512]{3,2,1,0:T(8,128)(2,1)}, bf16[1,2,64,512]{3,2,1,0:T(8,128)(2,1)}) custom-call(bf16[1,2,64,2048]{3,2,1,0:T(8,128)(2,1)} %inputs.1, bf16[1,2,64,512]{3,2,1,0:T(8,128)(2,1)} %keys.1, bf16[1,2,64,512]{3,2,1,0:T(8,128)(2,1)} %values.1, f32[1,2048]{1,0:T(1,128)} %gain_hbm.1, ...), custom_call_target="tpu_custom_call" | custom-call | tf_op jit(solution)/shard_map/plane_backward/pallas_call | solution.py:419
  39.0 25.0 %hand_out.1 = (bf16[1,2,64,2048]{3,2,1,0:T(8,128)(2,1)}, bf16[1,2,64,512]{3,2,1,0:T(8,128)(2,1)}, bf16[1,2,64,512]{3,2,1,0:T(8,128)(2,1)}) custom-call(bf16[1,2,64,2048]{3,2,1,0:T(8,128)(2,1)} %get-tuple-element.6.a, bf16[1,2,64,512]{3,2,1,0:T(8,128)(2,1)} %get-tuple-element.7.b, bf16[1,2,64,512]{3,2,1,0:T(8,128)(2,1)} %get-tuple-element.8.c), custom_call_target="tpu_custom_call" | custom-call | tf_op jit(solution)/shard_map/hand_out/pallas_call | solution.py:451

commit v3 on v2

--- a/solution.py
+++ b/solution.py
@@ -117,6 +117,16 @@
         for k in range(1, PLANE):
             arriving(t, kind, k).wait_recv()
 
+    def take_block(t, kind, b):
+        pl.when(me == b)(lambda: local(t, kind).wait())
+
+        @pl.when(me != b)
+        def _():
+            src, dst = pieces(t, me, b)[kind]
+            pltpu.make_async_remote_copy(
+                src, dst, plane_send.at[t, kind, 0], plane_recv.at[t, kind, b],
+                device_id=at(z, b), device_id_type=MESH).wait_recv()
+
     def finish_out(t, kind):
         for k in range(1, PLANE):
             remote(t, kind, k).wait_send()
@@ -158,8 +168,7 @@
 
     for t in range(ticks):
         exchange(t, (0, 1), start)
-        exchange(t, (2,), start)
-        exchange(t, (3,), start)
+    exchange(0, (2,), start)
 
     def near(t):
         return pltpu.make_async_remote_copy(
@@ -335,31 +344,33 @@
                 total_out(t, part, k).start()
             total_local(t, part).start()
 
-    send_keys(0)
     for t in range(ticks):
-        exchange(t, (2,), finish_in)
-        if t == 0:
-            finish_in(t, 3)
-        else:
-            pl.when(last)(lambda: finish_in(t, 3))
-
-            @pl.when(pp < n_pp - 1)
-            def _():
-                for b in range(PLANE):
-                    relay(t - 1, b).wait_recv()
+        send_keys(t)
+        if t > 0:
+            exchange(t, (2,), start)
+        exchange(t, (3,), start)
+    for t in range(ticks):
         take_keys(t)
         for b in range(PLANE):
+            take_block(t, 2, b)
+            if t == 0:
+                take_block(t, 3, b)
+            else:
+                pl.when(last)(lambda: take_block(t, 3, b))
+                pl.when(pp < n_pp - 1)(lambda: relay(t - 1, b).wait_recv())
             block_step(t, b)
-            if b == 0 and t + 1 < ticks:
-                send_keys(t + 1)
             if t + 1 < ticks:
                 pl.when(pp > 0)(lambda: relay(t, b).start())
-            pl.when(me != b)(lambda: result_out(t, b).start())
+            else:
+                pl.when(me != b)(lambda: result_out(t, b).start())
             if b * BLK + BLK == FAR:
                 stage[t, :, 0:FAR, :] = acc[t, :, 0:FAR, :].astype(jnp.bfloat16)
                 pl.when(z >= 2)(lambda: far_back(t).start())
             if t > 0 and b == PLANE - 2:
                 finish(t - 1)
+        if t + 1 < ticks:
+            for b in range(PLANE):
+                pl.when(me != b)(lambda: result_out(t, b).start())
         result_local(t).start()
         stage[t, :, FAR:PREV, :] = acc[t, :, FAR:PREV, :].astype(jnp.bfloat16)
         pl.when(z >= 1)(lambda: near_back(t).start())
@@ -445,16 +456,16 @@
             dma((ticks, 2, PLANE)), dma((ticks, 2, PLANE)),
         ],
         compiler_params=pltpu.CompilerParams(
-            collective_id=0, has_side_effects=True, vmem_limit_bytes=64 * 1024 * 1024),
+            collective_id=0, has_side_effects=True, vmem_limit_bytes=40 * 1024 * 1024),
         name="plane_backward",
-    )(inputs, keys, values, gain, first, head, window, stride)
+    )(*[pltpu.with_memory_space_constraint(a, pltpu.HBM) for a in (inputs, keys, values, gain, first, head, window, stride)])
     return pl.pallas_call(
         hand_out,
         out_shape=[jax.ShapeDtypeStruct(a.shape, bf16) for a in (inputs, keys, values)],
         in_specs=[anywhere] * 3,
         out_specs=[pl.BlockSpec(memory_space=pltpu.HBM)] * 3,
         scratch_shapes=[dma((3,))],
-        compiler_params=pltpu.CompilerParams(vmem_limit_bytes=64 * 1024 * 1024),
+        compiler_params=pltpu.CompilerParams(vmem_limit_bytes=40 * 1024 * 1024),
         name="hand_out",
     )(*outs)
 

time: 64.1 us -> 41.9 us (0.65)
  Pallas kernels: 63.3 us -> 41.1 us
    pallas_call x1, Pallas kernels: 25 us -> 0.9 us  [body(): pl.pallas_call(hand_out, out_shape=[jax.ShapeDtypeStruct(a.shape, bf16) f...]
    pallas_call x1, Pallas kernels: 38.4 us -> 40.2 us  [body(): pl.pallas_call(functools.partial(kernel, n_ctx, n_pp, ticks, group), out_...]
where the time goes in v3:
time: 41.9 us; the launch traced here: 41.7 us
  Pallas kernels  41.1 us (98%)
  between operations  0.64 us (2%)
    pallas_call x1, Pallas kernels, body(): pl.pallas_call(functools.partial(kernel, n_ctx, n_pp, ticks, group), out_...  40.2 us
    pallas_call x1, Pallas kernels, body(): pl.pallas_call(hand_out, out_shape=[jax.ShapeDtypeStruct(a.shape, bf16) f...  0.9 us

profile of v3, /device:TPU:0, one launch (start us, length us, event | category | flops | bytes accessed | tf_op | source)
XLA Modules:
  0.0 41.7 jit_solution(13548607781918119062)
XLA Ops:
  0.6 40.2 %plane_backward.1 = (bf16[1,2,64,2048]{3,2,1,0:T(8,128)(2,1)S(1)}, bf16[1,2,64,512]{3,2,1,0:T(8,128)(2,1)S(1)}, bf16[1,2,64,512]{3,2,1,0:T(8,128)(2,1)S(1)}) custom-call(bf16[1,2,64,2048]{3,2,1,0:T(8,128)(2,1)} %inputs.1, bf16[1,2,64,512]{3,2,1,0:T(8,128)(2,1)} %keys.1, bf16[1,2,64,512]{3,2,1,0:T(8,128)(2,1)} %values.1, f32[1,2048]{1,0:T(1,128)} %gain_hbm.1, ...), custom_call_target="tpu_custom_call" | custom-call | tf_op jit(solution)/shard_map/plane_backward/pallas_call | solution.py:430
  40.8 0.9 %hand_out.1 = (bf16[1,2,64,2048]{3,2,1,0:T(8,128)(2,1)}, bf16[1,2,64,512]{3,2,1,0:T(8,128)(2,1)}, bf16[1,2,64,512]{3,2,1,0:T(8,128)(2,1)}) custom-call(bf16[1,2,64,2048]{3,2,1,0:T(8,128)(2,1)S(1)} %get-tuple-element.6.a, bf16[1,2,64,512]{3,2,1,0:T(8,128)(2,1)S(1)} %get-tuple-element.7.b, bf16[1,2,64,512]{3,2,1,0:T(8,128)(2,1)S(1)} %get-tuple-element.8.c), custom_call_target="tpu_custom_call" | custom-call | tf_op jit(solution)/shard_map/hand_out/pallas_call | solution.py:462

commit v4 on v3

--- a/solution.py
+++ b/solution.py
@@ -16,6 +16,7 @@
 PREV = (WIN - 1) * BLK
 FAR = PREV - SPAN
 OWN = PREV
+PAIR_KEYS = WIN + 1
 STRIDED = PREV + SPAN
 MESH = pl.DeviceIdType.MESH
 LOG2E = 1.4426950408889634
@@ -34,6 +35,7 @@
     inputs, keys, values, gain_hbm, first, head, window_hbm, stride_hbm,
     grads_out, key_out, value_out,
     xq, gr, kv, res, acc, stage, near_in, far_in, strided_in, total, gain, window, stride, small_sem,
+    scores_at, grad_prob_at, probs_at, dscore_at,
     local_sem, plane_send, plane_recv, z_send, z_recv, str_send, str_recv,
     pass_send, pass_recv, res_send, res_recv,
     back_send, back_recv, sback_send, sback_recv, out_send, out_recv,
@@ -160,7 +162,8 @@
             for t in range(ticks):
                 kv[t, :, at_row:at_row + BLK, :] = zero((2, BLK, HEAD_DIM))
 
-    acc[...] = jnp.zeros_like(acc)
+    probs_at[...] = jnp.zeros_like(probs_at)
+    dscore_at[...] = jnp.zeros_like(dscore_at)
 
     pl.semaphore_wait(
         barrier,
@@ -168,7 +171,8 @@
 
     for t in range(ticks):
         exchange(t, (0, 1), start)
-    exchange(0, (2,), start)
+        exchange(t, (2,), start)
+        exchange(t, (3,), start)
 
     def near(t):
         return pltpu.make_async_remote_copy(
@@ -266,40 +270,80 @@
             allowed = on_stride * jnp.where(key_block <= block - WIN, 1, 0)
         return jnp.where(allowed == 1, jnp.float32(0), jnp.float32(-1e30))
 
-    def block_step(t, b):
-        block = z * PLANE + b
-        rows = slice(b * BLK, (b + 1) * BLK)
-        local_rows = slice(b * BLK, (b + WIN) * BLK)
+    def stack(matrix):
+        return jnp.concatenate([matrix[:, h * HEAD_DIM:(h + 1) * HEAD_DIM] for h in range(group)], axis=0)
+
+    def folded(chunk, combine):
+        return combine(chunk.reshape(BLK // 8, 8, lanes), axis=0)
+
+    lanes = group * BLK
+    factor = jnp.float32(scale * LOG2E)
+
+    def pair_step(t, pair):
+        first_row = pair * 2 * BLK
+        local_rows = slice(first_row, first_row + PAIR_KEYS * BLK)
         far_rows = slice(STRIDED, STRIDED + owners * BLK)
-        key_b = jnp.concatenate([kv[t, 0, local_rows, :], kv[t, 0, far_rows, :]], axis=0)
-        value_b = jnp.concatenate([kv[t, 1, local_rows, :], kv[t, 1, far_rows, :]], axis=0)
+        key_p = jnp.concatenate([kv[t, 0, local_rows, :], kv[t, 0, far_rows, :]], axis=0)
+        value_p = jnp.concatenate([kv[t, 1, local_rows, :], kv[t, 1, far_rows, :]], axis=0)
+        rows = slice(first_row, first_row + 2 * BLK)
         queries = (xq[t, rows, :].astype(jnp.float32) * my_gain).astype(jnp.bfloat16)
         grad = gr[t, rows, :]
-
-        def stack(matrix):
-            return jnp.concatenate([matrix[:, h * HEAD_DIM:(h + 1) * HEAD_DIM] for h in range(group)], axis=0)
-
-        query_b, grad_b = stack(queries), stack(grad)
-        scores = lax.dot_general(key_b, query_b, contract, preferred_element_type=jnp.float32)
-        scores = jnp.concatenate(
-            [rows_of(scores, c) + (causal if c == WIN - 1 else bias(block, c)) for c in range(WIN + owners)], axis=0)
-        peak = jnp.max(scores, axis=0, keepdims=True)
-        weights = jnp.exp2((scores - peak) * jnp.float32(scale * LOG2E))
-        inverse = 1.0 / jnp.sum(weights, axis=0, keepdims=True)
-        grad_prob = lax.dot_general(value_b, grad_b, contract, preferred_element_type=jnp.float32)
-        probs = weights * inverse
-        delta = jnp.sum(probs * grad_prob, axis=0, keepdims=True)
-        dscore = (probs * (grad_prob - delta) * jnp.float32(scale)).astype(jnp.bfloat16)
-        probs = probs.astype(jnp.bfloat16)
-        dquery = jnp.dot(key_b.T, dscore, preferred_element_type=jnp.float32).T
-        dquery = jnp.concatenate([rows_of(dquery, h) for h in range(group)], axis=1)
-        res[t, rows, :] = (grad.astype(jnp.float32) + my_gain * dquery).astype(jnp.bfloat16)
+        query_p = jnp.concatenate([stack(queries[:BLK]), stack(queries[BLK:])], axis=0)
+        grad_p = jnp.concatenate([stack(grad[:BLK]), stack(grad[BLK:])], axis=0)
+        scores_at[...] = lax.dot_general(key_p, query_p, contract, preferred_element_type=jnp.float32)
+        grad_prob_at[...] = lax.dot_general(value_p, grad_p, contract, preferred_element_type=jnp.float32)
+        for half in range(2):
+            block = z * PLANE + pair * 2 + half
+            cols = slice(half * lanes, (half + 1) * lanes)
+            chunks = [(c, c - half) for c in range(PAIR_KEYS) if 0 <= c - half < WIN]
+            chunks += [(PAIR_KEYS + q, WIN + q) for q in range(owners)]
+            biases = [None if kind == WIN - 1 else bias(block, kind) for c, kind in chunks]
+
+            def raw(c, kind):
+                chunk = scores_at[c * BLK:(c + 1) * BLK, cols]
+                return chunk + causal if kind == WIN - 1 else chunk
+
+            peak = None
+            for (c, kind), shift in zip(chunks, biases):
+                high = folded(raw(c, kind), jnp.max)
+                high = high if shift is None else high + shift
+                peak = high if peak is None else jnp.maximum(peak, high)
+            peak = jnp.max(peak, axis=0, keepdims=True) * factor
+            weight_sum = jnp.zeros((8, lanes), jnp.float32)
+            product_sum = jnp.zeros((8, lanes), jnp.float32)
+            for (c, kind), shift in zip(chunks, biases):
+                offset = -peak if shift is None else shift * factor - peak
+                weights = jnp.exp2(raw(c, kind) * factor + offset)
+                scores_at[c * BLK:(c + 1) * BLK, cols] = weights
+                weight_sum += folded(weights, jnp.sum)
+                product_sum += folded(weights * grad_prob_at[c * BLK:(c + 1) * BLK, cols], jnp.sum)
+            inverse = 1.0 / jnp.sum(weight_sum, axis=0, keepdims=True)
+            delta = jnp.sum(product_sum, axis=0, keepdims=True) * inverse
+            scaled = inverse * jnp.float32(scale)
+            for c, kind in chunks:
+                at_rows = slice(c * BLK, (c + 1) * BLK)
+                weights = scores_at[at_rows, cols]
+                probs_at[at_rows, cols] = (weights * inverse).astype(jnp.bfloat16)
+                dscore_at[at_rows, cols] = (
+                    (weights * scaled) * (grad_prob_at[at_rows, cols] - delta)).astype(jnp.bfloat16)
+        dscore = dscore_at[...]
+        dquery = jnp.dot(key_p.T, dscore, preferred_element_type=jnp.float32).T
+        for half in range(2):
+            mine = jnp.concatenate([rows_of(dquery, half * group + h) for h in range(group)], axis=1)
+            out_rows = slice(first_row + half * BLK, first_row + (half + 1) * BLK)
+            res[t, out_rows, :] = (gr[t, out_rows, :].astype(jnp.float32) + my_gain * mine).astype(jnp.bfloat16)
         for part, term in enumerate((
-            jnp.dot(dscore, query_b, preferred_element_type=jnp.float32),
-            jnp.dot(probs, grad_b, preferred_element_type=jnp.float32),
+            jnp.dot(dscore, query_p, preferred_element_type=jnp.float32),
+            jnp.dot(probs_at[...], grad_p, preferred_element_type=jnp.float32),
         )):
-            acc[t, part, local_rows, :] += term[:WIN * BLK]
-            acc[t, part, far_rows, :] += term[WIN * BLK:]
+            if pair == 0:
+                acc[t, part, local_rows, :] = term[:PAIR_KEYS * BLK]
+                acc[t, part, far_rows, :] = term[PAIR_KEYS * BLK:]
+            else:
+                seen = (PAIR_KEYS - 2) * BLK
+                acc[t, part, first_row:first_row + seen, :] += term[:seen]
+                acc[t, part, first_row + seen:first_row + seen + 2 * BLK, :] = term[seen:seen + 2 * BLK]
+                acc[t, part, far_rows, :] += term[PAIR_KEYS * BLK:]
 
     outs = (key_out, value_out)
 
@@ -344,32 +388,30 @@
                 total_out(t, part, k).start()
             total_local(t, part).start()
 
-    for t in range(ticks):
-        send_keys(t)
-        if t > 0:
-            exchange(t, (2,), start)
-        exchange(t, (3,), start)
+    send_keys(0)
     for t in range(ticks):
         take_keys(t)
-        for b in range(PLANE):
-            take_block(t, 2, b)
-            if t == 0:
-                take_block(t, 3, b)
-            else:
-                pl.when(last)(lambda: take_block(t, 3, b))
-                pl.when(pp < n_pp - 1)(lambda: relay(t - 1, b).wait_recv())
-            block_step(t, b)
+        for pair in range(PLANE // 2):
+            blocks = (2 * pair, 2 * pair + 1)
+            for b in blocks:
+                take_block(t, 2, b)
+                if t == 0:
+                    take_block(t, 3, b)
+                else:
+                    pl.when(last)(lambda: take_block(t, 3, b))
+                    pl.when(pp < n_pp - 1)(lambda: relay(t - 1, b).wait_recv())
+            pair_step(t, pair)
             if t + 1 < ticks:
-                pl.when(pp > 0)(lambda: relay(t, b).start())
-            else:
-                pl.when(me != b)(lambda: result_out(t, b).start())
-            if b * BLK + BLK == FAR:
+                for b in blocks:
+                    pl.when(pp > 0)(lambda: relay(t, b).start())
+            if pair == 0:
                 stage[t, :, 0:FAR, :] = acc[t, :, 0:FAR, :].astype(jnp.bfloat16)
                 pl.when(z >= 2)(lambda: far_back(t).start())
-            if t > 0 and b == PLANE - 2:
-                finish(t - 1)
-        if t + 1 < ticks:
-            for b in range(PLANE):
+                if t + 1 < ticks:
+                    send_keys(t + 1)
+                if t > 0:
+                    finish(t - 1)
+            for b in blocks:
                 pl.when(me != b)(lambda: result_out(t, b).start())
         result_local(t).start()
         stage[t, :, FAR:PREV, :] = acc[t, :, FAR:PREV, :].astype(jnp.bfloat16)
@@ -445,6 +487,10 @@
             pltpu.VMEM((ticks, 2, SPAN, HEAD_DIM), bf16),
             pltpu.VMEM(gain.shape, f32), pltpu.SMEM(window.shape, jnp.int32), pltpu.SMEM(stride.shape, jnp.int32),
             dma((3,)),
+            pltpu.VMEM(((PAIR_KEYS + owners) * BLK, 2 * group * BLK), f32),
+            pltpu.VMEM(((PAIR_KEYS + owners) * BLK, 2 * group * BLK), f32),
+            pltpu.VMEM(((PAIR_KEYS + owners) * BLK, 2 * group * BLK), bf16),
+            pltpu.VMEM(((PAIR_KEYS + owners) * BLK, 2 * group * BLK), bf16),
             dma((ticks, 7)),
             dma((ticks, 4, PLANE)), dma((ticks, 4, PLANE)),
             dma((ticks, 2)), dma((ticks, 2)),

time: 41.9 us -> 39.5 us (0.943)
  Pallas kernels: 41.1 us -> 38.7 us
    pallas_call x1, Pallas kernels: 40.2 us -> 37.8 us  [body(): pl.pallas_call(functools.partial(kernel, n_ctx, n_pp, ticks, group), out_...]
where the time goes in v4:
time: 39.5 us; the launch traced here: 39.3 us
  Pallas kernels  38.7 us (98%)
  between operations  0.64 us (2%)
    pallas_call x1, Pallas kernels, body(): pl.pallas_call(functools.partial(kernel, n_ctx, n_pp, ticks, group), out_...  37.8 us
    pallas_call x1, Pallas kernels, body(): pl.pallas_call(hand_out, out_shape=[jax.ShapeDtypeStruct(a.shape, bf16) f...  0.9 us

profile of v4, /device:TPU:0, one launch (start us, length us, event | category | flops | bytes accessed | tf_op | source)
XLA Modules:
  0.0 39.3 jit_solution(12177081791214642400)
XLA Ops:
  0.6 37.8 %plane_backward.1 = (bf16[1,2,64,2048]{3,2,1,0:T(8,128)(2,1)S(1)}, bf16[1,2,64,512]{3,2,1,0:T(8,128)(2,1)S(1)}, bf16[1,2,64,512]{3,2,1,0:T(8,128)(2,1)S(1)}) custom-call(bf16[1,2,64,2048]{3,2,1,0:T(8,128)(2,1)} %inputs.1, bf16[1,2,64,512]{3,2,1,0:T(8,128)(2,1)} %keys.1, bf16[1,2,64,512]{3,2,1,0:T(8,128)(2,1)} %values.1, f32[1,2048]{1,0:T(1,128)} %gain_hbm.1, ...), custom_call_target="tpu_custom_call" | custom-call | tf_op jit(solution)/shard_map/plane_backward/pallas_call | solution.py:472
  38.4 0.9 %hand_out.1 = (bf16[1,2,64,2048]{3,2,1,0:T(8,128)(2,1)}, bf16[1,2,64,512]{3,2,1,0:T(8,128)(2,1)}, bf16[1,2,64,512]{3,2,1,0:T(8,128)(2,1)}) custom-call(bf16[1,2,64,2048]{3,2,1,0:T(8,128)(2,1)S(1)} %get-tuple-element.6.a, bf16[1,2,64,512]{3,2,1,0:T(8,128)(2,1)S(1)} %get-tuple-element.7.b, bf16[1,2,64,512]{3,2,1,0:T(8,128)(2,1)S(1)} %get-tuple-element.8.c), custom_call_target="tpu_custom_call" | custom-call | tf_op jit(solution)/shard_map/hand_out/pallas_call | solution.py:508

commit v5 on v4

--- a/solution.py
+++ b/solution.py
@@ -169,10 +169,11 @@
         barrier,
         PLANE - 1 + planes - 1 + jnp.where(pp > 0, 1, 0) + jnp.where(last, 0, 1))
 
-    for t in range(ticks):
+    exchange(0, (0, 1), start)
+    exchange(0, (2,), start)
+    exchange(0, (3,), start)
+    for t in range(1, ticks):
         exchange(t, (0, 1), start)
-        exchange(t, (2,), start)
-        exchange(t, (3,), start)
 
     def near(t):
         return pltpu.make_async_remote_copy(
@@ -279,7 +280,7 @@
     lanes = group * BLK
     factor = jnp.float32(scale * LOG2E)
 
-    def pair_step(t, pair):
+    def pair_step(t, pair, send_terms):
         first_row = pair * 2 * BLK
         local_rows = slice(first_row, first_row + PAIR_KEYS * BLK)
         far_rows = slice(STRIDED, STRIDED + owners * BLK)
@@ -327,23 +328,34 @@
                 dscore_at[at_rows, cols] = (
                     (weights * scaled) * (grad_prob_at[at_rows, cols] - delta)).astype(jnp.bfloat16)
         dscore = dscore_at[...]
-        dquery = jnp.dot(key_p.T, dscore, preferred_element_type=jnp.float32).T
-        for half in range(2):
-            mine = jnp.concatenate([rows_of(dquery, half * group + h) for h in range(group)], axis=1)
-            out_rows = slice(first_row + half * BLK, first_row + (half + 1) * BLK)
-            res[t, out_rows, :] = (gr[t, out_rows, :].astype(jnp.float32) + my_gain * mine).astype(jnp.bfloat16)
-        for part, term in enumerate((
-            jnp.dot(dscore, query_p, preferred_element_type=jnp.float32),
-            jnp.dot(probs_at[...], grad_p, preferred_element_type=jnp.float32),
-        )):
-            if pair == 0:
-                acc[t, part, local_rows, :] = term[:PAIR_KEYS * BLK]
-                acc[t, part, far_rows, :] = term[PAIR_KEYS * BLK:]
-            else:
-                seen = (PAIR_KEYS - 2) * BLK
-                acc[t, part, first_row:first_row + seen, :] += term[:seen]
-                acc[t, part, first_row + seen:first_row + seen + 2 * BLK, :] = term[seen:seen + 2 * BLK]
-                acc[t, part, far_rows, :] += term[PAIR_KEYS * BLK:]
+        def queries_part():
+            dquery = jnp.dot(key_p.T, dscore, preferred_element_type=jnp.float32).T
+            for half in range(2):
+                mine = jnp.concatenate([rows_of(dquery, half * group + h) for h in range(group)], axis=1)
+                out_rows = slice(first_row + half * BLK, first_row + (half + 1) * BLK)
+                res[t, out_rows, :] = (gr[t, out_rows, :].astype(jnp.float32) + my_gain * mine).astype(jnp.bfloat16)
+
+        def keys_part():
+            for part, term in enumerate((
+                jnp.dot(dscore, query_p, preferred_element_type=jnp.float32),
+                jnp.dot(probs_at[...], grad_p, preferred_element_type=jnp.float32),
+            )):
+                if pair == 0:
+                    acc[t, part, local_rows, :] = term[:PAIR_KEYS * BLK]
+                    acc[t, part, far_rows, :] = term[PAIR_KEYS * BLK:]
+                else:
+                    seen = (PAIR_KEYS - 2) * BLK
+                    acc[t, part, first_row:first_row + seen, :] += term[:seen]
+                    acc[t, part, first_row + seen:first_row + seen + 2 * BLK, :] = term[seen:seen + 2 * BLK]
+                    acc[t, part, far_rows, :] += term[PAIR_KEYS * BLK:]
+
+        if send_terms is None:
+            queries_part()
+            keys_part()
+        else:
+            keys_part()
+            send_terms()
+            queries_part()
 
     outs = (key_out, value_out)
 
@@ -389,37 +401,49 @@
             total_local(t, part).start()
 
     send_keys(0)
+    for b in range(PLANE):
+        take_block(0, 2, b)
+        take_block(0, 3, b)
+    for t in range(1, ticks):
+        exchange(t, (2,), start)
+        exchange(t, (3,), start)
+    for t in range(1, ticks):
+        send_keys(t)
     for t in range(ticks):
         take_keys(t)
         for pair in range(PLANE // 2):
             blocks = (2 * pair, 2 * pair + 1)
-            for b in blocks:
-                take_block(t, 2, b)
-                if t == 0:
-                    take_block(t, 3, b)
-                else:
+            if t > 0:
+                for b in blocks:
+                    take_block(t, 2, b)
                     pl.when(last)(lambda: take_block(t, 3, b))
                     pl.when(pp < n_pp - 1)(lambda: relay(t - 1, b).wait_recv())
-            pair_step(t, pair)
+
+            def send_terms():
+                if pair == 0:
+                    stage[t, :, 0:FAR, :] = acc[t, :, 0:FAR, :].astype(jnp.bfloat16)
+                    pl.when(z >= 2)(lambda: far_back(t).start())
+                else:
+                    stage[t, :, FAR:PREV, :] = acc[t, :, FAR:PREV, :].astype(jnp.bfloat16)
+                    pl.when(z >= 1)(lambda: near_back(t).start())
+                    stage[t, :, STRIDED:, :] = acc[t, :, STRIDED:, :].astype(jnp.bfloat16)
+                    for q in range(owners):
+                        pl.when(z > step * q)(lambda: strided_back(t, q, z).start())
+
+            pair_step(t, pair, send_terms if t + 1 == ticks else None)
             if t + 1 < ticks:
                 for b in blocks:
                     pl.when(pp > 0)(lambda: relay(t, b).start())
-            if pair == 0:
-                stage[t, :, 0:FAR, :] = acc[t, :, 0:FAR, :].astype(jnp.bfloat16)
-                pl.when(z >= 2)(lambda: far_back(t).start())
-                if t + 1 < ticks:
-                    send_keys(t + 1)
-                if t > 0:
-                    finish(t - 1)
-            for b in blocks:
+                send_terms()
+            else:
+                for b in blocks:
+                    pl.when(me != b)(lambda: result_out(t, b).start())
+            if t > 0 and pair == 0:
+                finish(t - 1)
+        if t + 1 < ticks:
+            for b in range(PLANE):
                 pl.when(me != b)(lambda: result_out(t, b).start())
         result_local(t).start()
-        stage[t, :, FAR:PREV, :] = acc[t, :, FAR:PREV, :].astype(jnp.bfloat16)
-        pl.when(z >= 1)(lambda: near_back(t).start())
-        stage[t, :, STRIDED:, :] = acc[t, :, STRIDED:, :].astype(jnp.bfloat16)
-        for q in range(owners):
-            pl.when(z > step * q)(lambda: strided_back(t, q, z).start())
-
     finish(ticks - 1)
 
     for t in range(ticks):

time: 39.5 us -> 40.1 us (1.015)
  Pallas kernels: 38.7 us -> 39.3 us
    pallas_call x1, Pallas kernels: 37.8 us -> 38.4 us  [body(): pl.pallas_call(functools.partial(kernel, n_ctx, n_pp, ticks, group), out_...]
where the time goes in v5:
time: 40.1 us; the launch traced here: 39.9 us
  Pallas kernels  39.3 us (98%)
  between operations  0.64 us (2%)
    pallas_call x1, Pallas kernels, body(): pl.pallas_call(functools.partial(kernel, n_ctx, n_pp, ticks, group), out_...  38.4 us
    pallas_call x1, Pallas kernels, body(): pl.pallas_call(hand_out, out_shape=[jax.ShapeDtypeStruct(a.shape, bf16) f...  0.9 us

profile of v5, /device:TPU:0, one launch (start us, length us, event | category | flops | bytes accessed | tf_op | source)
XLA Modules:
  0.0 39.9 jit_solution(16143088710374641147)
XLA Ops:
  0.6 38.4 %plane_backward.1 = (bf16[1,2,64,2048]{3,2,1,0:T(8,128)(2,1)S(1)}, bf16[1,2,64,512]{3,2,1,0:T(8,128)(2,1)S(1)}, bf16[1,2,64,512]{3,2,1,0:T(8,128)(2,1)S(1)}) custom-call(bf16[1,2,64,2048]{3,2,1,0:T(8,128)(2,1)} %inputs.1, bf16[1,2,64,512]{3,2,1,0:T(8,128)(2,1)} %keys.1, bf16[1,2,64,512]{3,2,1,0:T(8,128)(2,1)} %values.1, f32[1,2048]{1,0:T(1,128)} %gain_hbm.1, ...), custom_call_target="tpu_custom_call" | custom-call | tf_op jit(solution)/shard_map/plane_backward/pallas_call | solution.py:496
  39.0 0.9 %hand_out.1 = (bf16[1,2,64,2048]{3,2,1,0:T(8,128)(2,1)}, bf16[1,2,64,512]{3,2,1,0:T(8,128)(2,1)}, bf16[1,2,64,512]{3,2,1,0:T(8,128)(2,1)}) custom-call(bf16[1,2,64,2048]{3,2,1,0:T(8,128)(2,1)S(1)} %get-tuple-element.6.a, bf16[1,2,64,512]{3,2,1,0:T(8,128)(2,1)S(1)} %get-tuple-element.7.b, bf16[1,2,64,512]{3,2,1,0:T(8,128)(2,1)S(1)} %get-tuple-element.8.c), custom_call_target="tpu_custom_call" | custom-call | tf_op jit(solution)/shard_map/hand_out/pallas_call | solution.py:532

commit v6 on v5

--- a/solution.py
+++ b/solution.py
@@ -182,8 +182,8 @@
 
     def far(t):
         return pltpu.make_async_remote_copy(
-            kv.at[t, :, OWN + SPAN - FAR:OWN + SPAN, :], kv.at[t, :, 0:FAR, :], z_send.at[t, 1], z_recv.at[t, 1],
-            device_id=at(z + 2, me), device_id_type=MESH)
+            kv.at[t, :, PREV - FAR:PREV, :], kv.at[t, :, 0:FAR, :], z_send.at[t, 1], z_recv.at[t, 1],
+            device_id=at(z + 1, me), device_id_type=MESH)
 
     def strided(t, q, plane):
         return pltpu.make_async_remote_copy(
@@ -194,20 +194,26 @@
         for q in range(owners):
             @pl.when(z == step * q)
             def _():
-                for plane in range(step * q + 1, planes):
+                for plane in range(step * q + 2, planes):
                     act(q, plane)
 
     def send_keys(t):
         exchange(t, (0, 1), finish_in)
         pl.when(z + 1 < planes)(lambda: near(t).start())
-        pl.when(z + 2 < planes)(lambda: far(t).start())
         each_strided(lambda q, plane: strided(t, q, plane).start())
 
+    def pass_keys(t):
+        pl.when(z >= 1)(lambda: near(t).wait_recv())
+        pl.when((z >= 1) & (z + 1 < planes))(lambda: far(t).start())
+        for q in range(owners):
+            @pl.when(z == step * q + 1)
+            def _():
+                kv[t, :, STRIDED + q * BLK:STRIDED + (q + 1) * BLK, :] = kv[t, :, FAR:FAR + BLK, :]
+
     def take_keys(t):
-        pl.when(z >= 1)(lambda: near(t).wait_recv())
         pl.when(z >= 2)(lambda: far(t).wait_recv())
         for q in range(owners):
-            pl.when(z > step * q)(lambda: strided(t, q, 0).wait_recv())
+            pl.when(z > step * q + 1)(lambda: strided(t, q, 0).wait_recv())
 
     def result_out(t, b):
         return pltpu.make_async_remote_copy(
@@ -238,7 +244,7 @@
     def far_back(t):
         return pltpu.make_async_remote_copy(
             stage.at[t, :, 0:FAR, :], far_in.at[t], back_send.at[t, 1], back_recv.at[t, 1],
-            device_id=at(z - 2, me), device_id_type=MESH)
+            device_id=at(z - 1, me), device_id_type=MESH)
 
     def strided_back(t, q, plane):
         return pltpu.make_async_remote_copy(
@@ -384,11 +390,6 @@
             near_back(t).wait_recv()
             acc[t, :, OWN:OWN + SPAN, :] += near_in[t].astype(jnp.float32)
 
-        @pl.when(z + 2 < planes)
-        def _():
-            far_back(t).wait_recv()
-            acc[t, :, OWN + SPAN - FAR:OWN + SPAN, :] += far_in[t].astype(jnp.float32)
-
         def add_strided(q, plane):
             strided_back(t, q, plane).wait_recv()
             acc[t, :, OWN:OWN + BLK, :] += strided_in[t, plane].astype(jnp.float32)
@@ -401,6 +402,7 @@
             total_local(t, part).start()
 
     send_keys(0)
+    pass_keys(0)
     for b in range(PLANE):
         take_block(0, 2, b)
         take_block(0, 3, b)
@@ -424,17 +426,30 @@
                     stage[t, :, 0:FAR, :] = acc[t, :, 0:FAR, :].astype(jnp.bfloat16)
                     pl.when(z >= 2)(lambda: far_back(t).start())
                 else:
+                    @pl.when((z >= 1) & (z + 1 < planes))
+                    def _():
+                        far_back(t).wait_recv()
+                        acc[t, :, PREV - FAR:PREV, :] += far_in[t].astype(jnp.float32)
+
+                    for q in range(owners):
+                        @pl.when(z == step * q + 1)
+                        def _():
+                            slot = STRIDED + q * BLK
+                            acc[t, :, FAR:FAR + BLK, :] += acc[t, :, slot:slot + BLK, :]
+
                     stage[t, :, FAR:PREV, :] = acc[t, :, FAR:PREV, :].astype(jnp.bfloat16)
                     pl.when(z >= 1)(lambda: near_back(t).start())
                     stage[t, :, STRIDED:, :] = acc[t, :, STRIDED:, :].astype(jnp.bfloat16)
                     for q in range(owners):
-                        pl.when(z > step * q)(lambda: strided_back(t, q, z).start())
+                        pl.when(z > step * q + 1)(lambda: strided_back(t, q, z).start())
 
             pair_step(t, pair, send_terms if t + 1 == ticks else None)
             if t + 1 < ticks:
                 for b in blocks:
                     pl.when(pp > 0)(lambda: relay(t, b).start())
                 send_terms()
+                if pair == 0:
+                    pass_keys(t + 1)
             else:
                 for b in blocks:
                     pl.when(me != b)(lambda: result_out(t, b).start())
@@ -450,7 +465,7 @@
         exchange(t, (0, 1, 2), finish_out)
         exchange(t, (3,), finish_out)
         pl.when(z + 1 < planes)(lambda: near(t).wait_send())
-        pl.when(z + 2 < planes)(lambda: far(t).wait_send())
+        pl.when((z >= 1) & (z + 1 < planes))(lambda: far(t).wait_send())
         each_strided(lambda q, plane: strided(t, q, plane).wait_send())
         for b in range(PLANE):
             if t + 1 < ticks:
@@ -459,7 +474,7 @@
         pl.when(z >= 2)(lambda: far_back(t).wait_send())
         pl.when(z >= 1)(lambda: near_back(t).wait_send())
         for q in range(owners):
-            pl.when(z > step * q)(lambda: strided_back(t, q, z).wait_send())
+            pl.when(z > step * q + 1)(lambda: strided_back(t, q, z).wait_send())
         result_local(t).wait()
         for k in range(1, PLANE):
             result_in(t, lax.rem(me + k, PLANE)).wait_recv()

time: 40.1 us -> 41.8 us (1.042)
  Pallas kernels: 39.3 us -> 41 us
    pallas_call x1, Pallas kernels: 38.4 us -> 40.1 us  [body(): pl.pallas_call(functools.partial(kernel, n_ctx, n_pp, ticks, group), out_...]
where the time goes in v6:
time: 41.8 us; the launch traced here: 41.6 us
  Pallas kernels  41 us (98%)
  between operations  0.64 us (2%)
    pallas_call x1, Pallas kernels, body(): pl.pallas_call(functools.partial(kernel, n_ctx, n_pp, ticks, group), out_...  40.1 us
    pallas_call x1, Pallas kernels, body(): pl.pallas_call(hand_out, out_shape=[jax.ShapeDtypeStruct(a.shape, bf16) f...  0.9 us

profile of v6, /device:TPU:0, one launch (start us, length us, event | category | flops | bytes accessed | tf_op | source)
XLA Modules:
  0.0 41.6 jit_solution(14637594466859269996)
XLA Ops:
  0.6 40.1 %plane_backward.1 = (bf16[1,2,64,2048]{3,2,1,0:T(8,128)(2,1)S(1)}, bf16[1,2,64,512]{3,2,1,0:T(8,128)(2,1)S(1)}, bf16[1,2,64,512]{3,2,1,0:T(8,128)(2,1)S(1)}) custom-call(bf16[1,2,64,2048]{3,2,1,0:T(8,128)(2,1)} %inputs.1, bf16[1,2,64,512]{3,2,1,0:T(8,128)(2,1)} %keys.1, bf16[1,2,64,512]{3,2,1,0:T(8,128)(2,1)} %values.1, f32[1,2048]{1,0:T(1,128)} %gain_hbm.1, ...), custom_call_target="tpu_custom_call" | custom-call | tf_op jit(solution)/shard_map/plane_backward/pallas_call | solution.py:511
  40.7 0.9 %hand_out.1 = (bf16[1,2,64,2048]{3,2,1,0:T(8,128)(2,1)}, bf16[1,2,64,512]{3,2,1,0:T(8,128)(2,1)}, bf16[1,2,64,512]{3,2,1,0:T(8,128)(2,1)}) custom-call(bf16[1,2,64,2048]{3,2,1,0:T(8,128)(2,1)S(1)} %get-tuple-element.6.a, bf16[1,2,64,512]{3,2,1,0:T(8,128)(2,1)S(1)} %get-tuple-element.7.b, bf16[1,2,64,512]{3,2,1,0:T(8,128)(2,1)S(1)} %get-tuple-element.8.c), custom_call_target="tpu_custom_call" | custom-call | tf_op jit(solution)/shard_map/hand_out/pallas_call | solution.py:547
